TPU v7x, 256 devices: a whole 4x4x8 slice. The times are simulated.
256 devices in a mesh: dp: 8 (over z), expert: 8 (over y, core), tensor: 4 (over x).
Axes of the slice: x: 4, y: 4, z: 8, core: 2. Of those that a mesh axis runs over, the one named last changes fastest.
Arguments:
- tokens: bfloat16 [1024, 6144], P('dp', 'expert'), may hold values from -6 to 6
- out_grad: bfloat16 [1024, 6144], P('dp', 'expert'), may hold values from -3 to 3
- expert_ids: int32 [1024, 2], P('dp'), may hold values from 0 to 7, all different within a row; in each aligned block of 128 rows (0 to 127, 128 to 255, ...) at most 48 rows name the same one
- combine_weights: float32 [1024, 2], P('dp'), may hold values from 0.05 to 1
- w_gate: bfloat16 [8, 6144, 8192], P('expert', None, ('dp', 'tensor')), may hold values from -0.078125 to 0.078125
- w_up: bfloat16 [8, 6144, 8192], P('expert', None, ('dp', 'tensor')), may hold values from -0.078125 to 0.078125
- w_down: bfloat16 [8, 8192, 6144], P('expert', ('dp', 'tensor')), may hold values from -0.0625 to 0.0625
Outputs:
- x_grad: bfloat16 [1024, 6144], P('dp', 'expert')
- router_grad: float32 [1024, 2], P('dp')
Inputs may be any that keep to these rules, and one draw needn't show every extreme that they name: `expert_ids`: in each aligned block of 128 tokens (the tokens of one index of dp) at most 48 entries name one expert, a bound that the crowded blocks reach; the two experts of a token differ.
All inputs are finite; a program needn't handle non-finite values.
Results may differ from a plain program's by a relative error of at most 0.0049.
Values may be sent and summed in bfloat16 or wider, within the bound.
No kernel may reach another device: no remote copies, remote signals or barrier semaphores. Data moves between devices by JAX's collectives and lax.ppermute only.
A program may use at most 128 MiB of HBM per device.

v0:
```python
import jax
import jax.numpy as jnp
from jax import lax
from jax.sharding import PartitionSpec as P

EXPERTS = 8


def expert_terms(rows_input, rows_cotangent, w_gate, w_up, w_down):
    gate_value = jnp.einsum("lrd,ldf->lrf", rows_input, w_gate, preferred_element_type=jnp.float32)
    up_value = jnp.einsum("lrd,ldf->lrf", rows_input, w_up, preferred_element_type=jnp.float32)
    sigmoid_gate = jax.nn.sigmoid(gate_value)
    activation = gate_value * sigmoid_gate
    hidden_value = activation * up_value
    backward = jnp.einsum(
        "lrd,lfd->lrf", rows_cotangent, w_down, preferred_element_type=jnp.float32
    )
    slot_part = jnp.sum(backward * hidden_value, axis=2)
    grad_up = (backward * activation).astype(jnp.bfloat16)
    grad_gate = (
        backward * up_value * sigmoid_gate * (1.0 + gate_value * (1.0 - sigmoid_gate))
    ).astype(jnp.bfloat16)
    grad_part = jnp.einsum("lrf,ldf->lrd", grad_gate, w_gate, preferred_element_type=jnp.float32)
    grad_part = grad_part + jnp.einsum(
        "lrf,ldf->lrd", grad_up, w_up, preferred_element_type=jnp.float32
    )
    return (grad_part, slot_part)


def per_device(tokens, out_grad, expert_ids, combine_weights, w_gate, w_up, w_down):
    token_count, part_width = tokens.shape
    expert_devices = lax.axis_size("expert")
    local_count = w_gate.shape[0]
    capacity = 3 * token_count // EXPERTS
    flat_ids = expert_ids.reshape(-1)
    expert_range = jnp.arange(EXPERTS, dtype=jnp.int32)
    one_hot = (flat_ids[:, None] == expert_range[None, :]).astype(jnp.int32)
    earlier = jnp.cumsum(one_hot, axis=0) - one_hot
    slot_index = jnp.sum(earlier * one_hot, axis=1)
    flat_row = flat_ids * capacity + slot_index
    token_index = jnp.arange(token_count * 2, dtype=jnp.int32) // 2
    row_table = (
        jnp.full((EXPERTS * capacity,), token_count, jnp.int32).at[flat_row].set(token_index)
    )
    zero_row = jnp.zeros((1, part_width), tokens.dtype)
    padded_input = jnp.concatenate([tokens, zero_row], axis=0)
    padded_cotangent = jnp.concatenate([out_grad, zero_row], axis=0)
    send_input = padded_input[row_table].reshape(expert_devices, local_count, capacity, part_width)
    send_cotangent = padded_cotangent[row_table].reshape(
        expert_devices, local_count, capacity, part_width
    )
    recv_input, recv_cotangent = (
        lax.all_to_all(send_input, "expert", split_axis=0, concat_axis=3, tiled=True),
        lax.all_to_all(send_cotangent, "expert", split_axis=0, concat_axis=3, tiled=True),
    )
    rows_input, rows_cotangent = (
        lax.all_gather(recv_input[0], "dp", axis=1, tiled=True),
        lax.all_gather(recv_cotangent[0], "dp", axis=1, tiled=True),
    )
    grad_part, slot_part = expert_terms(rows_input, rows_cotangent, w_gate, w_up, w_down)
    grad_rows, slot_rows = (
        lax.psum_scatter(grad_part, ("dp", "tensor"), scatter_dimension=1, tiled=True),
        lax.psum_scatter(slot_part, ("dp", "tensor"), scatter_dimension=1, tiled=True),
    )
    quarter_rows = grad_rows.shape[1]
    back_input = grad_rows.reshape(local_count, quarter_rows, expert_devices, part_width)
    back_slots = jnp.broadcast_to(
        slot_rows[:, :, None, None], (local_count, quarter_rows, expert_devices, 1)
    )
    ret_input, ret_slots = (
        lax.all_to_all(back_input, "expert", split_axis=2, concat_axis=0, tiled=True),
        lax.all_to_all(back_slots, "expert", split_axis=2, concat_axis=0, tiled=True),
    )
    ret_input = ret_input.reshape(EXPERTS, quarter_rows, part_width)
    ret_slots = ret_slots.reshape(EXPERTS, quarter_rows)
    flat_weights = combine_weights.reshape(-1)
    full_input, full_slots = (
        lax.all_gather(ret_input, "tensor", axis=1, tiled=True),
        lax.all_gather(ret_slots, "tensor", axis=1, tiled=True),
    )
    picked = full_input.reshape(-1, part_width)[flat_row] * flat_weights[:, None]
    token_grad = jnp.sum(picked.reshape(token_count, 2, part_width), axis=1)
    router_grad = full_slots.reshape(-1)[flat_row].reshape(token_count, 2)
    return (token_grad.astype(jnp.bfloat16), router_grad)


def solution(mesh):
    placed = (
        P("dp", "expert"),
        P("dp", "expert"),
        P("dp", None),
        P("dp", None),
        P("expert", None, ("dp", "tensor")),
        P("expert", None, ("dp", "tensor")),
        P("expert", ("dp", "tensor"), None),
    )
    return jax.shard_map(
        per_device,
        mesh=mesh,
        in_specs=placed,
        out_specs=(P("dp", "expert"), P("dp", None)),
        check_vma=False,
    )
```

profile of v0, /device:TPU:1, one launch (start us, length us, event | category | flops | bytes accessed | tf_op | source)
XLA Modules:
  0.0 540.7 jit_solution(5573689254099451336)
XLA Ops:
  12.7 2.6 gather_fusion.1
  15.4 17.2 %all_to_all.60 = bf16[8,1,48,768]{3,2,1,0:T(8,128)(2,1)S(1)} all-to-all(bf16[8,1,48,768]{3,2,1,0:T(8,128)(2,1)} %bitcast.81), channel_id=1, replica_groups=mesh['dp'=8,'expert'=8,'tensor'=4] {'expert'}, dimensions={0} | all-to-all | bytes 1179648 | tf_op jit(solution)/shard_map/all_to_all | solution.py:53
  33.5 2.1 squeeze.7
  35.8 2.7 gather_fusion
  38.4 14.5 %all_to_all.61 = bf16[8,1,48,768]{3,2,1,0:T(8,128)(2,1)S(1)} all-to-all(bf16[8,1,48,768]{3,2,1,0:T(8,128)(2,1)} %bitcast.80), channel_id=1, replica_groups=mesh['dp'=8,'expert'=8,'tensor'=4] {'expert'}, dimensions={0} | all-to-all | bytes 1179648 | tf_op jit(solution)/shard_map/all_to_all | solution.py:54
  54.0 2.1 squeeze.6
  56.4 39.5 %all-gather.8.cloned.1.call-done = bf16[1,384,6144]{2,1,0:T(8,128)(2,1)} async-done(((bf16[1,48,6144]{2,1,0:T(8,128)(2,1)}), bf16[1,384,6144]{2,1,0:T(8,128)(2,1)}) %all-gather.8.cloned.1.call-update) | async-done | bytes 4718608 | tf_op jit(solution)/shard_map/all_gather | solution.py:57
  95.9 4.3 fusion
  100.6 2.6 fusion.2
  103.2 52.9 %all-gather.6.cloned.1.call-done = bf16[1,384,6144]{2,1,0:T(8,128)(2,1)} async-done(((bf16[1,48,6144]{2,1,0:T(8,128)(2,1)}), bf16[1,384,6144]{2,1,0:T(8,128)(2,1)}) %all-gather.6.cloned.1.call-update) | async-done | bytes 4718608 | tf_op jit(solution)/shard_map/all_gather | solution.py:58
  156.0 5.2 multiply_reduce_fusion.1
  164.6 24.5 %copy.40 = f32[1,384,6144]{2,0,1:T(1,128)} copy(f32[1,384,6144]{2,1,0:T(8,128)S(1)} %add_bitcast_fusion) | data formatting | bytes 18874368 | tf_op jit(solution)/shard_map/add | solution.py:24
  191.0 221.8 %all-reduce.6.cloned.1.call-done = f32[1,384,6144]{2,0,1:T(1,128)} async-done(((f32[1,384,6144]{2,0,1:T(1,128)}), f32[1,384,6144]{2,0,1:T(1,128)}) %all-reduce.6.cloned.1.call-update) | async-done | bytes 9437200
  412.8 1.7 dynamic-slice_reduce_fusion
  415.0 12.1 %all_to_all.62 = f32[1,12,8,768]{3,0,1,2:T(1,128)S(1)} all-to-all(f32[1,12,8,768]{3,0,1,2:T(1,128)S(1)} %copy.41), channel_id=1, replica_groups=mesh['dp'=8,'expert'=8,'tensor'=4] {'expert'}, dimensions={2} | all-to-all | bytes 589824 | tf_op jit(solution)/shard_map/all_to_all | solution.py:71
  427.9 59.1 %all-reduce.3 = f32[1,384]{1,0:T(1,128)S(1)} all-reduce(f32[1,384]{1,0:T(1,128)S(1)} %reduce_sum.35), channel_id=5, replica_groups=mesh['dp'=8,'expert'=8,'tensor'=4] {'dp','tensor'}, use_global_device_ids=true, to_apply=%region_7.8.clone | all-reduce | flops 384 | bytes 3072
  487.7 18.0 %all-to-all-start.3 = ((f32[1,12,8,1]{1,3,0,2:T(1,128)}), f32[1,12,8,1]{1,3,0,2:T(1,128)S(1)}, u32[]{:S(2)}, u32[]{:S(2)}) async-start(f32[1,12,8,1]{1,3,0,2:T(1,128)} %broadcast_in_dim.11), calls=%async_computation.3 | async-start | bytes 8192 | tf_op jit(solution)/shard_map/all_to_all | solution.py:72
  505.8 4.4 all-to-all-done.3
  510.3 9.2 %all-gather.1 = f32[8,1,48,1,1]{0,4,3,1,2:T(1,128)S(1)} all-gather(f32[8,1,12,1,1]{0,4,3,1,2:T(1,128)S(1)} %copy.46), channel_id=3, replica_groups=mesh['dp'=8,'expert'=8,'tensor'=4] {'tensor'}, dimensions={2}, use_global_device_ids=true | all-gather | bytes 1920 | tf_op jit(solution)/shard_map/all_gather | solution.py:79
  519.7 2.0 gather_fusion.3
  522.4 2.7 copy.44
  525.1 3.7 gather_fusion.2
  528.8 2.5 gather.17
  531.3 2.8 multiply_reduce_fusion
  (69 shorter events, 15.8 us)
Async XLA Ops:
  7.2 88.7 %copy-start = (bf16[1,6144,256]{2,1,0:T(8,128)(2,1)S(1)}, bf16[1,6144,256]{2,1,0:T(8,128)(2,1)}, u32[]{:S(2)}) copy-start(bf16[1,6144,256]{2,1,0:T(8,128)(2,1)} %param.11) | copy-start | bytes 9437188
  7.2 88.7 %all-gather.8.cloned.1.call-start = ((), (), s32[]{:S(2)}) async-start(), calls=%async_computation.5 | async-start | bytes 5308416 | tf_op jit(solution)/shard_map/all_gather | solution.py:57
  10.3 1.4 copy-start.6
  15.4 20.4 %copy-start.5 = (bf16[128,768]{1,0:T(8,128)(2,1)S(1)}, bf16[128,768]{1,0:T(8,128)(2,1)}, u32[]{:S(2)}) copy-start(bf16[128,768]{1,0:T(8,128)(2,1)} %param.8) | copy-start | bytes 589828
  35.7 120.3 %all-gather.6.cloned.1.call-start = ((), (), s32[]{:S(2)}) async-start(), calls=%async_computation.4 | async-start | bytes 5308416 | tf_op jit(solution)/shard_map/all_gather | solution.py:58
  56.1 356.7 %all-reduce.6.cloned.1.call-start = ((), (), s32[]{:S(2)}) async-start(), calls=%async_computation.7 | async-start | bytes 18874368
  95.9 4.3 copy-start.2
  95.9 4.7 copy-start.9
  156.0 5.2 copy-start.4
  161.2 1.9 copy-start.3
  189.1 0.7 copy-start.10
  189.1 316.6 %copy-start.7 = (s32[256,1]{0,1:T(1,128)S(1)}, s32[256,1]{0,1:T(1,128)}, u32[]{:S(2)}) copy-start(s32[256,1]{0,1:T(1,128)} %copy-done.6) | copy-start | bytes 3076
  189.1 316.6 %copy-start.8 = (f32[128,2]{0,1:T(2,128)S(1)}, f32[128,2]{0,1:T(2,128)}, u32[]{:S(2)}) copy-start(f32[128,2]{0,1:T(2,128)} %param.10) | copy-start | bytes 3076
  189.1 333.3 %all-gather.10.cloned.1.call-start = ((), (), s32[]{:S(2)}) async-start(), calls=%async_computation.6 | async-start | bytes 1474560 | tf_op jit(solution)/shard_map/all_gather | solution.py:78
  487.7 22.5 %all-to-all-start.3 = ((f32[1,12,8,1]{1,3,0,2:T(1,128)}), f32[1,12,8,1]{1,3,0,2:T(1,128)S(1)}, u32[]{:S(2)}, u32[]{:S(2)}) async-start(f32[1,12,8,1]{1,3,0,2:T(1,128)} %broadcast_in_dim.11), calls=%async_computation.3 | async-start | bytes 8192 | tf_op jit(solution)/shard_map/all_to_all | solution.py:72
  525.1 9.0 %copy-start.1 = (bf16[1,6144,256]{2,1,0:T(8,128)(2,1)S(1)}, bf16[1,6144,256]{2,1,0:T(8,128)(2,1)}, u32[]{:S(2)}) copy-start(bf16[1,6144,256]{2,1,0:T(8,128)(2,1)} %param.11) | copy-start | bytes 9437188
Sparse Core Ops, SparseCore 0:
  35.8 60.0 all-gather.7
  97.7 58.3 all-gather.5
  189.2 223.5 all-reduce.5
  428.0 22.9 all-gather.9
where the time goes:
time: 542 us; the launch traced here: 541 us
  waiting for transfers between devices  319 us (59%)
  blocking collectives  112 us (21%)
  local copies, waits for them, and re-layouts  57.6 us (11%)
  starting transfers between devices  18.3 us (3%)
  matrix products  15 us (3%)
  between operations  14.6 us (3%)
    unnamed x5, waiting for transfers between devices  222 us
    unnamed x1, blocking collectives  59.1 us
    all_gather x1, waiting for transfers between devices, per_device(): lax.all_gather(recv_cotangent[0], 'dp', axis=1, tiled=True)  52.9 us
    all_gather x1, waiting for transfers between devices, per_device(): lax.all_gather(recv_input[0], 'dp', axis=1, tiled=True)  39.5 us
    add x1, local copies, waits for them, and re-layouts, expert_terms(): grad_part + jnp.einsum('lrf,ldf->lrd', grad_up, w_up, preferred_element_t...  24.5 us
    all_to_all x1, starting transfers between devices, per_device(): lax.all_to_all(back_slots, 'expert', split_axis=2, concat_axis=0, tiled=T...  18 us
    all_to_all x1, blocking collectives, per_device(): lax.all_to_all(send_input, 'expert', split_axis=0, concat_axis=3, tiled=T...  17.2 us
    all_to_all x1, blocking collectives, per_device(): lax.all_to_all(send_cotangent, 'expert', split_axis=0, concat_axis=3, til...  14.5 us
  transfers between devices with their start and end apart: 5, of which 4 were waited for; matrix products, arithmetic and copies ran while one was open for 3% of the time, Pallas kernels for 0%

commit v1 on v0

v1 whole, which is shorter than its diff:
```python
import functools

import jax
import jax.numpy as jnp
from jax import lax
from jax.experimental import pallas as pl
from jax.experimental.pallas import tpu as pltpu
from jax.sharding import PartitionSpec as P

EXPERTS = 8
CAP = 48
BF = jnp.bfloat16
F32 = jnp.float32
HIGH = lax.Precision.HIGHEST


def nt(a, b, **kw):
    return lax.dot_general(a, b, (((1,), (1,)), ((), ())), preferred_element_type=F32, **kw)


def tn(a, b, **kw):
    return lax.dot_general(a, b, (((0,), (0,)), ((), ())), preferred_element_type=F32, **kw)


def slot_masks(ids):
    tokens = ids.shape[1]
    experts = lax.broadcasted_iota(jnp.int32, (EXPERTS, tokens), 0)
    ind0 = (ids[0:1, :] == experts).astype(F32)
    ind1 = (ids[1:2, :] == experts).astype(F32)
    before = (
        lax.broadcasted_iota(jnp.int32, (tokens, tokens), 0)
        < lax.broadcasted_iota(jnp.int32, (tokens, tokens), 1)
    )
    count = jnp.dot((ind0 + ind1).astype(BF), before.astype(BF), preferred_element_type=F32)
    return ind0, ind1, count.astype(jnp.int32)


def dispatch_kernel(ids_ref, tok_ref, og_ref, out_ref):
    ind0, ind1, count = slot_masks(ids_ref[...])
    ind = ind0 + ind1
    tokens = ind.shape[1]
    slots = lax.broadcasted_iota(jnp.int32, (CAP, tokens), 0)
    for e in range(EXPERTS):
        pick = jnp.where(count[e : e + 1, :] == slots, ind[e : e + 1, :], 0.0).astype(BF)
        out_ref[e, 0:CAP, :] = jnp.dot(pick, tok_ref[...], preferred_element_type=F32).astype(BF)
        out_ref[e, CAP : 2 * CAP, :] = jnp.dot(
            pick, og_ref[...], preferred_element_type=F32
        ).astype(BF)


def dispatch(ids, tokens, out_grad):
    width = tokens.shape[1]
    return pl.pallas_call(
        dispatch_kernel,
        out_shape=jax.ShapeDtypeStruct((EXPERTS, 2 * CAP, width), BF),
        compiler_params=pltpu.CompilerParams(vmem_limit_bytes=24 << 20),
        name="dispatch",
    )(ids, tokens, out_grad)


def forward_kernel(count, halves, *refs):
    n_in = 2 if halves else count
    ins = refs[:n_in]
    wg_ref, wu_ref, wd_ref = refs[n_in : n_in + 3]
    outs = refs[n_in + 3 : n_in + 3 + 2 * count]
    acc_g, acc_u, acc_b = refs[n_in + 3 + 2 * count :]
    e = pl.program_id(0)

    @pl.when(e == 0)
    def _():
        acc_g[...] = jnp.zeros_like(acc_g)
        acc_u[...] = jnp.zeros_like(acc_u)
        acc_b[...] = jnp.zeros_like(acc_b)

    if halves:
        blocks = [jnp.where(e < EXPERTS // 2, ins[0][0], ins[1][0])]
    else:
        blocks = [r[0] for r in ins]
    tok = jnp.concatenate([b[:CAP] for b in blocks], axis=0)
    og = jnp.concatenate([b[CAP:] for b in blocks], axis=0)
    acc_g[...] += jnp.dot(tok, wg_ref[0], preferred_element_type=F32)
    acc_u[...] += jnp.dot(tok, wu_ref[0], preferred_element_type=F32)
    acc_b[...] += nt(og, wd_ref[0])

    @pl.when(e == EXPERTS - 1)
    def _():
        gate, up, back = acc_g[...], acc_u[...], acc_b[...]
        sig = jax.nn.sigmoid(gate)
        act = gate * sig
        prod = back * (act * up)
        grad_up = (back * act).astype(BF)
        grad_gate = (back * up * sig * (1.0 + gate * (1.0 - sig))).astype(BF)
        hidden = gate.shape[1]
        ones = jnp.ones((16, hidden), F32)
        fill = jnp.zeros((128 - CAP, hidden), F32)
        for i in range(count):
            rows = slice(i * CAP, (i + 1) * CAP)
            outs[2 * i][:, :hidden] = grad_gate[rows]
            outs[2 * i][:, hidden:] = grad_up[rows]
            outs[2 * i + 1][...] = nt(
                ones, jnp.concatenate([prod[rows], fill], axis=0), precision=HIGH
            )


def forward(blocks, halves, w_gate, w_up, w_down):
    hidden = w_gate.shape[2]
    width = blocks[0].shape[2]
    count = 1 if halves else len(blocks)
    shape = (1, 2 * CAP, width)
    if halves:
        last = EXPERTS // 2 - 1
        in_specs = [
            pl.BlockSpec(shape, lambda e: (jnp.minimum(e, last), 0, 0)),
            pl.BlockSpec(shape, lambda e: (jnp.maximum(e - last - 1, 0), 0, 0)),
        ]
    else:
        in_specs = [pl.BlockSpec(shape, lambda e: (e, 0, 0)) for _ in blocks]
    in_specs += [
        pl.BlockSpec((1, width, hidden), lambda e: (0, e, 0)),
        pl.BlockSpec((1, width, hidden), lambda e: (0, e, 0)),
        pl.BlockSpec((1, hidden, width), lambda e: (0, 0, e)),
    ]
    rows = count * CAP
    outs = pl.pallas_call(
        functools.partial(forward_kernel, count, halves),
        grid=(EXPERTS,),
        in_specs=in_specs,
        out_specs=[
            pl.BlockSpec((CAP, 2 * hidden), lambda e: (0, 0)),
            pl.BlockSpec((16, 128), lambda e: (0, 0)),
        ]
        * count,
        out_shape=[
            jax.ShapeDtypeStruct((CAP, 2 * hidden), BF),
            jax.ShapeDtypeStruct((16, 128), F32),
        ]
        * count,
        scratch_shapes=[pltpu.VMEM((rows, hidden), F32)] * 3,
        compiler_params=pltpu.CompilerParams(vmem_limit_bytes=24 << 20),
        cost_estimate=pl.CostEstimate(
            flops=6 * 256 * EXPERTS * width * hidden,
            bytes_accessed=6 * EXPERTS * width * hidden,
            transcendentals=0,
        ),
        name="forward",
    )(*blocks, w_gate, w_up, w_down)
    return [(outs[2 * i], outs[2 * i + 1]) for i in range(count)]


def pack_slots(total, width):
    high = total.astype(BF).astype(F32)
    low = total - high
    row = lax.broadcasted_iota(jnp.int32, (16, 128), 0)
    packed = jnp.where(row == 0, high, jnp.where(row == 1, low, 0.0)).astype(BF)
    return jnp.concatenate([packed, jnp.zeros((16, width - 128), BF)], axis=1)


def unpack_slots(rows):
    packed = rows.astype(F32)
    return packed[0:1] + packed[1:2]


def backward_kernel(dist, *refs):
    e = pl.program_id(0)
    half = EXPERTS // 2
    if dist == 4:
        g_ref, s_ref, wg_ref, wu_ref, plus_ref, minus_ref = refs
    elif dist == 0:
        g_ref, s_ref, rp_ref, rm_ref, wg_ref, wu_ref, out_ref = refs
    else:
        gp_ref, sp_ref, gm_ref, sm_ref, rp_ref, rm_ref, wg_ref, wu_ref, plus_ref, minus_ref = refs
    hidden = wg_ref.shape[2]
    width = wg_ref.shape[1]

    def product(grads):
        return nt(grads[:, :hidden], wg_ref[0]) + nt(grads[:, hidden:], wu_ref[0])

    if dist == 4:
        part = product(g_ref[...]).astype(BF)

        @pl.when(e == 0)
        def _():
            plus_ref[0:16, :] = pack_slots(s_ref[0:1, :], width)

        @pl.when(e < half)
        def _():
            plus_ref[pl.ds(pl.multiple_of(16 + e * CAP, 16), CAP), :] = part

        @pl.when(e >= half)
        def _():
            minus_ref[pl.ds(pl.multiple_of((e - half) * CAP, 16), CAP), :] = part

    elif dist == 3:
        part = product(jnp.concatenate([gp_ref[...], gm_ref[...]], axis=0))
        place = pl.ds(pl.multiple_of(16 + e * CAP, 16), CAP)

        @pl.when(e == 0)
        def _():
            plus_ref[0:16, :] = pack_slots(
                sp_ref[0:1, :] + unpack_slots(rp_ref[0:16, 0:128]), width
            )
            minus_ref[0:16, :] = pack_slots(sm_ref[0:1, :], width)

        @pl.when(e < half)
        def _():
            plus_ref[place, :] = (part[:CAP] + rp_ref[place, :].astype(F32)).astype(BF)
            minus_ref[place, :] = part[CAP:].astype(BF)

        @pl.when(e >= half)
        def _():
            from_minus = rm_ref[pl.ds(pl.multiple_of((e - half) * CAP, 16), CAP), :].astype(F32)
            plus_ref[place, :] = part[:CAP].astype(BF)
            minus_ref[place, :] = (part[CAP:] + from_minus).astype(BF)

    elif dist == 0:
        place = pl.ds(pl.multiple_of(16 + e * CAP, 16), CAP)
        part = product(g_ref[...])
        part = part + (rp_ref[place, :].astype(F32) + rm_ref[place, :].astype(F32))
        out_ref[0, 0:CAP, :] = part.astype(BF)
        total = s_ref[0:1, :] + (
            unpack_slots(rp_ref[0:16, 0:128]) + unpack_slots(rm_ref[0:16, 0:128])
        )
        out_ref[0, CAP : CAP + 16, :] = pack_slots(total, width)
    else:
        part = product(jnp.concatenate([gp_ref[...], gm_ref[...]], axis=0))
        place = pl.ds(pl.multiple_of(16 + e * CAP, 16), CAP)

        @pl.when(e == 0)
        def _():
            plus_ref[0:16, :] = pack_slots(
                sp_ref[0:1, :] + unpack_slots(rp_ref[0:16, 0:128]), width
            )
            minus_ref[0:16, :] = pack_slots(
                sm_ref[0:1, :] + unpack_slots(rm_ref[0:16, 0:128]), width
            )

        plus_ref[place, :] = (part[:CAP] + rp_ref[place, :].astype(F32)).astype(BF)
        minus_ref[place, :] = (part[CAP:] + rm_ref[place, :].astype(F32)).astype(BF)


def backward(dist, small, received, w_gate, w_up):
    hidden = w_gate.shape[2]
    width = w_gate.shape[1] // EXPERTS
    half_rows = CAP * EXPERTS // 2
    full = 16 + CAP * EXPERTS

    def whole(a):
        return pl.BlockSpec(a.shape, lambda e: (0,) * len(a.shape))

    if dist == 4:
        shapes = [(16 + half_rows, width), (half_rows, width)]
    elif dist == 0:
        shapes = [(EXPERTS, CAP + 16, width)]
    else:
        shapes = [(full, width), (full, width)]
    out_shape = [jax.ShapeDtypeStruct(s, BF) for s in shapes]
    if dist == 0:
        out_specs = [pl.BlockSpec((1, CAP + 16, width), lambda e: (e, 0, 0))]
    else:
        out_specs = [whole(s) for s in out_shape]
    return pl.pallas_call(
        functools.partial(backward_kernel, dist),
        grid=(EXPERTS,),
        in_specs=[whole(a) for a in (*small, *received)]
        + [pl.BlockSpec((1, width, hidden), lambda e: (0, e, 0))] * 2,
        out_specs=out_specs,
        out_shape=out_shape,
        compiler_params=pltpu.CompilerParams(vmem_limit_bytes=24 << 20),
        cost_estimate=pl.CostEstimate(
            flops=4 * 256 * EXPERTS * width * hidden,
            bytes_accessed=4 * EXPERTS * width * hidden,
            transcendentals=0,
        ),
        name="backward",
    )(*small, *received, w_gate, w_up)


def combine_kernel(ids_ref, weight_ref, rows_ref, out_ref):
    ind0, ind1, count = slot_masks(ids_ref[...])
    tokens = ind0.shape[1]
    width = rows_ref.shape[2]
    weights = weight_ref[...]
    scale = ind0 * weights[0:1, :] + ind1 * weights[1:2, :]
    slots = lax.broadcasted_iota(jnp.int32, (CAP, tokens), 0)
    total = jnp.zeros((tokens, width), F32)
    router0 = jnp.zeros((16, tokens), F32)
    router1 = jnp.zeros((16, tokens), F32)
    for e in range(EXPERTS):
        here = count[e : e + 1, :] == slots
        pick = jnp.where(here, scale[e : e + 1, :], 0.0)
        total += tn(pick, rows_ref[e, 0:CAP, :].astype(F32), precision=HIGH)
        slot_rows = rows_ref[e, CAP : CAP + 16, 0:128][:, :CAP].astype(F32)
        one0 = jnp.where(here, ind0[e : e + 1, :], 0.0)
        one1 = jnp.where(here, ind1[e : e + 1, :], 0.0)
        router0 += jnp.dot(slot_rows, one0, precision=HIGH, preferred_element_type=F32)
        router1 += jnp.dot(slot_rows, one1, precision=HIGH, preferred_element_type=F32)
    out_ref[0:tokens, :] = total.astype(BF)
    sum0 = router0[0:1] + router0[1:2]
    sum1 = router1[0:1] + router1[1:2]
    high0, high1 = sum0.astype(BF).astype(F32), sum1.astype(BF).astype(F32)
    row = lax.broadcasted_iota(jnp.int32, (16, tokens), 0)
    packed = jnp.where(row == 0, high0, 0.0) + jnp.where(row == 1, sum0 - high0, 0.0)
    packed = packed + jnp.where(row == 2, high1, 0.0) + jnp.where(row == 3, sum1 - high1, 0.0)
    out_ref[tokens : tokens + 16, :] = jnp.concatenate(
        [packed.astype(BF), jnp.zeros((16, width - tokens), BF)], axis=1
    )


def combine(ids, weights, rows):
    tokens = ids.shape[1]
    return pl.pallas_call(
        combine_kernel,
        out_shape=jax.ShapeDtypeStruct((tokens + 16, rows.shape[2]), BF),
        compiler_params=pltpu.CompilerParams(vmem_limit_bytes=24 << 20),
        name="combine",
    )(ids, weights, rows)


def finish_kernel(a_ref, b_ref, c_ref, d_ref, x_ref, r_ref):
    tokens = x_ref.shape[0]
    total = (a_ref[...].astype(F32) + c_ref[...].astype(F32)) + (
        b_ref[...].astype(F32) + d_ref[...].astype(F32)
    )
    x_ref[...] = total[:tokens].astype(BF)
    tail = total[tokens : tokens + 16, :tokens]
    r_ref[0:1, :] = tail[0:1] + tail[1:2]
    r_ref[1:2, :] = tail[2:3] + tail[3:4]


def finish(own, plus, two, minus):
    tokens = own.shape[0] - 16
    return pl.pallas_call(
        finish_kernel,
        out_shape=(
            jax.ShapeDtypeStruct((tokens, own.shape[1]), BF),
            jax.ShapeDtypeStruct((2, tokens), F32),
        ),
        compiler_params=pltpu.CompilerParams(vmem_limit_bytes=24 << 20),
        name="finish",
    )(own, plus, two, minus)


def shift(a, axis, by):
    n = lax.axis_size(axis)
    return lax.ppermute(a, axis, [(i, (i + by) % n) for i in range(n)])


def per_device(tokens, out_grad, expert_ids, combine_weights, w_gate, w_up, w_down):
    ids = expert_ids.T
    weights = combine_weights.T
    half = EXPERTS // 2
    send = dispatch(ids, tokens, out_grad)
    own = lax.all_to_all(send, "expert", split_axis=0, concat_axis=0)
    up, down = own, own
    grads = {}
    blocks = {0: [own]}
    for dist in range(1, 4):
        up, down = shift(up, "dp", 1), shift(down, "dp", -1)
        blocks[dist] = [down, up]
    blocks[4] = [shift(up[:half], "dp", 1), shift(down[half:], "dp", -1)]
    for dist in range(5):
        grads[dist] = forward(blocks[dist], dist == 4, w_gate, w_up, w_down)
    received = ()
    for dist in range(4, 0, -1):
        small = [a for pair in grads[dist] for a in pair]
        plus, minus = backward(dist, small, received, w_gate, w_up)
        received = (shift(plus, "dp", 1), shift(minus, "dp", -1))
    (rows,) = backward(0, list(grads[0][0]), received, w_gate, w_up)
    rows = lax.all_to_all(rows, "expert", split_axis=0, concat_axis=0)
    part = combine(ids, weights, rows)
    x_grad, router = finish(
        part, shift(part, "tensor", 1), shift(part, "tensor", 2), shift(part, "tensor", -1)
    )
    return x_grad, router.T


def solution(mesh):
    placed = (
        P("dp", "expert"),
        P("dp", "expert"),
        P("dp", None),
        P("dp", None),
        P("expert", None, ("dp", "tensor")),
        P("expert", None, ("dp", "tensor")),
        P("expert", ("dp", "tensor"), None),
    )
    return jax.shard_map(
        per_device,
        mesh=mesh,
        in_specs=placed,
        out_specs=(P("dp", "expert"), P("dp", None)),
        check_vma=False,
    )
```

time: 542 us -> 225 us (0.42)
  waiting for transfers between devices: 319 us -> 105 us
  blocking collectives: 112 us -> 46.6 us
  local copies, waits for them, and re-layouts: 57.6 us -> 4.51 us
  Pallas kernels: 0 us -> 38.1 us
  matrix products: 15 us -> 0 us
  between operations: 14.6 us -> 0.79 us
  starting transfers between devices: 18.3 us -> 29.9 us
    unnamed x5 -> x0, waiting for transfers between devices: 222 us -> none
    ppermute x0 -> x19, waiting for transfers between devices: none -> 105 us  [shift(): return lax.ppermute(a, axis, [(i, (i + by) % n) for i in range(n)])]
    all_gather x3 -> x0, waiting for transfers between devices: 92.4 us -> none  [the longest x1 52.9 us: per_device(): lax.all_gather(recv_cotangent[0], 'dp', axis=1, tiled=True)]
    unnamed x1 -> x0, blocking collectives: 59.1 us -> none
    pallas_call x0 -> x13, Pallas kernels: none -> 38.1 us  [the longest x5 17.9 us: forward(): pl.pallas_call(functools.partial(forward_kernel, count, halves), grid=(EX...]
    ppermute x0 -> x19, starting transfers between devices: none -> 29.9 us  [shift(): return lax.ppermute(a, axis, [(i, (i + by) % n) for i in range(n)])]
    add x1 -> x0, local copies, waits for them, and re-layouts: 24.5 us -> none  [expert_terms(): grad_part + jnp.einsum('lrf,ldf->lrd', grad_up, w_up, preferred_element_t...]
    all_to_all x1 -> x0, starting transfers between devices: 18 us -> none  [per_device(): lax.all_to_all(back_slots, 'expert', split_axis=2, concat_axis=0, tiled=T...]
  transfers between devices with their start and end apart: 5 -> 19, of which waited for: 4 -> 10; matrix products, arithmetic and copies ran while one was open for 3% -> 0% of each run, Pallas kernels for 0% -> 6%
where the time goes in v1:
time: 225 us
  waiting for transfers between devices  105 us (47%)
  blocking collectives  46.6 us (21%)
  Pallas kernels  38.1 us (17%)
  starting transfers between devices  29.9 us (13%)
  local copies, waits for them, and re-layouts  4.51 us (2%)
    ppermute x19, waiting for transfers between devices, shift(): return lax.ppermute(a, axis, [(i, (i + by) % n) for i in range(n)])  105 us
    ppermute x19, starting transfers between devices, shift(): return lax.ppermute(a, axis, [(i, (i + by) % n) for i in range(n)])  29.9 us
    all_to_all x1, blocking collectives, per_device(): rows = lax.all_to_all(rows, 'expert', split_axis=0, concat_axis=0)  23.9 us
    all_to_all x1, blocking collectives, per_device(): own = lax.all_to_all(send, 'expert', split_axis=0, concat_axis=0)  22.7 us
    pallas_call x5, Pallas kernels, forward(): pl.pallas_call(functools.partial(forward_kernel, count, halves), grid=(EX...  17.9 us
    pallas_call x5, Pallas kernels, backward(): pl.pallas_call(functools.partial(backward_kernel, dist), grid=(EXPERTS,),...  15.5 us
  transfers between devices with their start and end apart: 19, of which 10 were waited for; matrix products, arithmetic and copies ran while one was open for 0% of the time, Pallas kernels for 6%

profile of v1, /device:TPU:1, one launch (start us, length us, event | category | flops | bytes accessed | tf_op | source)
XLA Modules:
  0.0 224.9 jit_solution(18017075332049438862)
XLA Ops:
  3.9 22.7 %all_to_all.10.refs_0_ = bf16[8,96,768]{2,1,0:T(8,128)(2,1)S(1)} all-to-all(bf16[8,96,768]{2,1,0:T(8,128)(2,1)S(1)} %dispatch.1), channel_id=1, replica_groups=mesh['dp'=8,'expert'=8,'tensor'=4] {'expert'}, dimensions={0} | all-to-all | bytes 2359296 | tf_op jit(solution)/shard_map/all_to_all | solution.py:353
  28.2 3.9 %collective-permute-start = (bf16[8,96,768]{2,1,0:T(8,128)(2,1)S(1)}, bf16[8,96,768]{2,1,0:T(8,128)(2,1)S(1)}, u32[]{:S(2)}, u32[]{:S(2)}) collective-permute-start(bf16[8,96,768]{2,1,0:T(8,128)(2,1)S(1)} %all_to_all.10.refs_0_), channel_id=1, source_target_pairs={{0,224},{32,0},{64,32},{96,64},{128,96},{160,128},{192,160},{224,1... | collective-permute-start | bytes 3538952 | tf_op jit(solution)/shard_map/ppermute | solution.py:345
  32.1 25.5 %collective-permute-done.1.refs_1_ = bf16[8,96,768]{2,1,0:T(8,128)(2,1)S(1)} collective-permute-done((bf16[8,96,768]{2,1,0:T(8,128)(2,1)S(1)}, bf16[8,96,768]{2,1,0:T(8,128)(2,1)S(1)}, u32[]{:S(2)}, u32[]{:S(2)}) %collective-permute-start.1) | collective-permute-done | bytes 1179680 | tf_op jit(solution)/shard_map/ppermute | solution.py:345
  57.6 2.7 %collective-permute-start.2 = (bf16[8,96,768]{2,1,0:T(8,128)(2,1)S(1)}, bf16[8,96,768]{2,1,0:T(8,128)(2,1)S(1)}, u32[]{:S(2)}, u32[]{:S(2)}) collective-permute-start(bf16[8,96,768]{2,1,0:T(8,128)(2,1)S(1)} %collective-permute-done.refs_0_), channel_id=1, source_target_pairs={{0,224},{32,0},{64,32},{96,64},{128,96},{160,128},{192,160},{224,1... | collective-permute-start | bytes 3538952 | tf_op jit(solution)/shard_map/ppermute | solution.py:345
  60.3 24.5 %collective-permute-done.3.refs_1_ = bf16[8,96,768]{2,1,0:T(8,128)(2,1)S(1)} collective-permute-done((bf16[8,96,768]{2,1,0:T(8,128)(2,1)S(1)}, bf16[8,96,768]{2,1,0:T(8,128)(2,1)S(1)}, u32[]{:S(2)}, u32[]{:S(2)}) %collective-permute-start.3) | collective-permute-done | bytes 1179680 | tf_op jit(solution)/shard_map/ppermute | solution.py:345
  87.5 23.6 %collective-permute-done.5.refs_1_ = bf16[8,96,768]{2,1,0:T(8,128)(2,1)S(1)} collective-permute-done((bf16[8,96,768]{2,1,0:T(8,128)(2,1)S(1)}, bf16[8,96,768]{2,1,0:T(8,128)(2,1)S(1)}, u32[]{:S(2)}, u32[]{:S(2)}) %collective-permute-start.5) | collective-permute-done | bytes 1179680 | tf_op jit(solution)/shard_map/ppermute | solution.py:345
  111.3 2.7 %collective-permute-start.7 = (bf16[4,96,768]{2,1,0:T(8,128)(2,1)S(1)}, bf16[4,96,768]{2,1,0:T(8,128)(2,1)S(1)}, u32[]{:S(2)}, u32[]{:S(2)}) collective-permute-start(bf16[4,96,768]{2,1,0:T(8,128)(2,1)S(1)} %slice.9), channel_id=1, source_target_pairs={{0,224},{32,0},{64,32},{96,64},{128,96},{160,128},{192,160},{224,1... | collective-permute-start | bytes 1769480 | tf_op jit(solution)/shard_map/ppermute | solution.py:345
  114.0 9.9 %collective-permute-done.6.refs_0_ = bf16[4,96,768]{2,1,0:T(8,128)(2,1)S(1)} collective-permute-done((bf16[4,96,768]{2,1,0:T(8,128)(2,1)S(1)}, bf16[4,96,768]{2,1,0:T(8,128)(2,1)S(1)}, u32[]{:S(2)}, u32[]{:S(2)}) %collective-permute-start.6) | collective-permute-done | bytes 589856 | tf_op jit(solution)/shard_map/ppermute | solution.py:345
  125.9 3.5 %forward.9 = (bf16[48,512]{1,0:T(8,128)(2,1)S(1)}, f32[16,128]{1,0:T(8,128)S(1)}) custom-call(bf16[4,96,768]{2,1,0:T(8,128)(2,1)S(1)} %collective-permute-done.6.refs_0_, bf16[4,96,768]{2,1,0:T(8,128)(2,1)S(1)} %collective-permute-done.7.refs_1_, bf16[1,6144,256]{2,1,0:T(8,128)(2,1)S(1)} %copy-done, bf16[1,6144,256]{2,1,0:T(8,128)(2,1)S(1)} %copy-done.1, ...), custom_call_target="tpu_custom_call" | custom-call | flops 2415919104 | bytes 9437184 | tf_op jit(solution)/shard_map/forward/pallas_call | solution.py:124
  129.4 2.9 %backward.5 = (bf16[208,768]{1,0:T(8,128)(2,1)S(1)}, bf16[192,768]{1,0:T(8,128)(2,1)S(1)}) custom-call(bf16[48,512]{1,0:T(8,128)(2,1)S(1)} %get-tuple-element.42.refs_0_, f32[16,128]{1,0:T(8,128)S(1)} %get-tuple-element.43.refs_1_, bf16[1,6144,256]{2,1,0:T(8,128)(2,1)S(1)} %copy-done, bf16[1,6144,256]{2,1,0:T(8,128)(2,1)S(1)} %copy-done.1), custom_call_target="tpu_custom_call" | custom-call | flops 1610612736 | bytes 6291456 | tf_op jit(solution)/shard_map/backward/pallas_call | solution.py:261
  135.1 3.7 %forward.8 = (bf16[48,512]{1,0:T(8,128)(2,1)S(1)}, f32[16,128]{1,0:T(8,128)S(1)}, bf16[48,512]{1,0:T(8,128)(2,1)S(1)}, f32[16,128]{1,0:T(8,128)S(1)}) custom-call(bf16[8,96,768]{2,1,0:T(8,128)(2,1)S(1)} %collective-permute-done.4.refs_0_, bf16[8,96,768]{2,1,0:T(8,128)(2,1)S(1)} %collective-permute-done.5.refs_1_, bf16[1,6144,256]{2,1,0:T(8,128)(2,1)S(1)} %copy-done, ...), custom_call_target="tpu_custom_call" | custom-call | flops 2415919104 | bytes 9437184 | tf_op jit(solution)/shard_map/forward/pallas_call | solution.py:124
  139.4 3.2 %backward.6 = (bf16[400,768]{1,0:T(8,128)(2,1)S(1)}, bf16[400,768]{1,0:T(8,128)(2,1)S(1)}) custom-call(bf16[48,512]{1,0:T(8,128)(2,1)S(1)} %get-tuple-element.38.refs_0_, f32[16,128]{1,0:T(8,128)S(1)} %get-tuple-element.39.refs_1_, bf16[48,512]{1,0:T(8,128)(2,1)S(1)} %get-tuple-element.40.refs_2_, f32[16,128]{1,0:T(8,128)S(1)} %get-tuple-element.41.refs_3_, ...), custom_call_target="tpu_custom_call" | custom-call | flops 1610612736 | bytes 6291456 | tf_op jit(solution)/shard_map/backward/pallas_call | solution.py:261
  145.4 3.7 %forward.7 = (bf16[48,512]{1,0:T(8,128)(2,1)S(1)}, f32[16,128]{1,0:T(8,128)S(1)}, bf16[48,512]{1,0:T(8,128)(2,1)S(1)}, f32[16,128]{1,0:T(8,128)S(1)}) custom-call(bf16[8,96,768]{2,1,0:T(8,128)(2,1)S(1)} %collective-permute-done.2.refs_0_, bf16[8,96,768]{2,1,0:T(8,128)(2,1)S(1)} %collective-permute-done.3.refs_1_, bf16[1,6144,256]{2,1,0:T(8,128)(2,1)S(1)} %copy-done, ...), custom_call_target="tpu_custom_call" | custom-call | flops 2415919104 | bytes 9437184 | tf_op jit(solution)/shard_map/forward/pallas_call | solution.py:124
  149.1 4.8 %collective-permute-done.10.refs_4_ = bf16[400,768]{1,0:T(8,128)(2,1)S(1)} collective-permute-done((bf16[400,768]{1,0:T(8,128)(2,1)S(1)}, bf16[400,768]{1,0:T(8,128)(2,1)S(1)}, u32[]{:S(2)}, u32[]{:S(2)}) %collective-permute-start.10) | collective-permute-done | bytes 614432 | tf_op jit(solution)/shard_map/ppermute | solution.py:345
  153.9 3.3 %backward.7 = (bf16[400,768]{1,0:T(8,128)(2,1)S(1)}, bf16[400,768]{1,0:T(8,128)(2,1)S(1)}) custom-call(bf16[48,512]{1,0:T(8,128)(2,1)S(1)} %get-tuple-element.34.refs_0_, f32[16,128]{1,0:T(8,128)S(1)} %get-tuple-element.35.refs_1_, bf16[48,512]{1,0:T(8,128)(2,1)S(1)} %get-tuple-element.36.refs_2_, f32[16,128]{1,0:T(8,128)S(1)} %get-tuple-element.37.refs_3_, ...), custom_call_target="tpu_custom_call" | custom-call | flops 1610612736 | bytes 6291456 | tf_op jit(solution)/shard_map/backward/pallas_call | solution.py:261
  160.1 3.7 %forward.6 = (bf16[48,512]{1,0:T(8,128)(2,1)S(1)}, f32[16,128]{1,0:T(8,128)S(1)}, bf16[48,512]{1,0:T(8,128)(2,1)S(1)}, f32[16,128]{1,0:T(8,128)S(1)}) custom-call(bf16[8,96,768]{2,1,0:T(8,128)(2,1)S(1)} %collective-permute-done.refs_0_, bf16[8,96,768]{2,1,0:T(8,128)(2,1)S(1)} %collective-permute-done.1.refs_1_, bf16[1,6144,256]{2,1,0:T(8,128)(2,1)S(1)} %copy-done, ...), custom_call_target="tpu_custom_call" | custom-call | flops 2415919104 | bytes 9437184 | tf_op jit(solution)/shard_map/forward/pallas_call | solution.py:124
  163.8 3.9 %collective-permute-done.12.refs_4_ = bf16[400,768]{1,0:T(8,128)(2,1)S(1)} collective-permute-done((bf16[400,768]{1,0:T(8,128)(2,1)S(1)}, bf16[400,768]{1,0:T(8,128)(2,1)S(1)}, u32[]{:S(2)}, u32[]{:S(2)}) %collective-permute-start.12) | collective-permute-done | bytes 614432 | tf_op jit(solution)/shard_map/ppermute | solution.py:345
  167.7 3.3 %backward.8 = (bf16[400,768]{1,0:T(8,128)(2,1)S(1)}, bf16[400,768]{1,0:T(8,128)(2,1)S(1)}) custom-call(bf16[48,512]{1,0:T(8,128)(2,1)S(1)} %get-tuple-element.30.refs_0_, f32[16,128]{1,0:T(8,128)S(1)} %get-tuple-element.31.refs_1_, bf16[48,512]{1,0:T(8,128)(2,1)S(1)} %get-tuple-element.32.refs_2_, f32[16,128]{1,0:T(8,128)S(1)} %get-tuple-element.33.refs_3_, ...), custom_call_target="tpu_custom_call" | custom-call | flops 1610612736 | bytes 6291456 | tf_op jit(solution)/shard_map/backward/pallas_call | solution.py:261
  173.8 3.4 %forward.5 = (bf16[48,512]{1,0:T(8,128)(2,1)S(1)}, f32[16,128]{1,0:T(8,128)S(1)}) custom-call(bf16[8,96,768]{2,1,0:T(8,128)(2,1)S(1)} %all_to_all.10.refs_0_, bf16[1,6144,256]{2,1,0:T(8,128)(2,1)S(1)} %copy-done, bf16[1,6144,256]{2,1,0:T(8,128)(2,1)S(1)} %copy-done.1, bf16[1,256,6144]{2,1,0:T(8,128)(2,1)S(1)} %copy-done.3), custom_call_target="tpu_custom_call" | custom-call | flops 2415919104 | bytes 9437184 | tf_op jit(solution)/shard_map/forward/pallas_call | solution.py:124
  177.2 4.0 %collective-permute-done.14.refs_2_ = bf16[400,768]{1,0:T(8,128)(2,1)S(1)} collective-permute-done((bf16[400,768]{1,0:T(8,128)(2,1)S(1)}, bf16[400,768]{1,0:T(8,128)(2,1)S(1)}, u32[]{:S(2)}, u32[]{:S(2)}) %collective-permute-start.14) | collective-permute-done | bytes 614432 | tf_op jit(solution)/shard_map/ppermute | solution.py:345
  181.2 2.8 %backward.9 = bf16[8,64,768]{2,1,0:T(8,128)(2,1)S(1)} custom-call(bf16[48,512]{1,0:T(8,128)(2,1)S(1)} %get-tuple-element.28.refs_0_, f32[16,128]{1,0:T(8,128)S(1)} %get-tuple-element.29.refs_1_, bf16[400,768]{1,0:T(8,128)(2,1)S(1)} %collective-permute-done.14.refs_2_, bf16[400,768]{1,0:T(8,128)(2,1)S(1)} %collective-permute-done.15.refs_3_, ...), custom_call_target="tpu_custom_call" | custom-call | flops 1610612736 | bytes 6291456 | tf_op jit(solution)/shard_map/backward/pallas_call | solution.py:261
  184.1 23.9 %all_to_all.11.rows_ref = bf16[8,64,768]{2,1,0:T(8,128)(2,1)S(1)} all-to-all(bf16[8,64,768]{2,1,0:T(8,128)(2,1)S(1)} %backward.9), channel_id=1, replica_groups=mesh['dp'=8,'expert'=8,'tensor'=4] {'expert'}, dimensions={0} | all-to-all | bytes 1572864 | tf_op jit(solution)/shard_map/all_to_all | solution.py:369
  208.0 3.2 %combine.1.a_ref = bf16[144,768]{1,0:T(8,128)(2,1)S(1)} custom-call(s32[2,128]{1,0:T(2,128)S(1)} %bitcast.4, f32[2,128]{1,0:T(2,128)S(1)} %bitcast.5, bf16[8,64,768]{2,1,0:T(8,128)(2,1)S(1)} %all_to_all.11.rows_ref), custom_call_target="tpu_custom_call" | custom-call | tf_op jit(solution)/shard_map/combine/pallas_call | solution.py:311
  218.4 5.7 %collective-permute-done.17.c_ref = bf16[144,768]{1,0:T(8,128)(2,1)S(1)} collective-permute-done((bf16[144,768]{1,0:T(8,128)(2,1)S(1)}, bf16[144,768]{1,0:T(8,128)(2,1)S(1)}, u32[]{:S(2)}, u32[]{:S(2)}) %collective-permute-start.17) | collective-permute-done | bytes 221216 | tf_op jit(solution)/shard_map/ppermute | solution.py:345
  (49 shorter events, 29.5 us)
Async XLA Ops:
  3.2 120.8 %copy-start.1 = (bf16[1,6144,256]{2,1,0:T(8,128)(2,1)S(1)}, bf16[1,6144,256]{2,1,0:T(8,128)(2,1)}, u32[]{:S(2)}) copy-start(bf16[1,6144,256]{2,1,0:T(8,128)(2,1)} %refs_5_.1) | copy-start | bytes 9437188
  3.9 120.1 %copy-start = (bf16[1,6144,256]{2,1,0:T(8,128)(2,1)S(1)}, bf16[1,6144,256]{2,1,0:T(8,128)(2,1)}, u32[]{:S(2)}) copy-start(bf16[1,6144,256]{2,1,0:T(8,128)(2,1)} %refs_4_.9) | copy-start | bytes 9437188
  26.5 31.0 %collective-permute-start.1 = (bf16[8,96,768]{2,1,0:T(8,128)(2,1)S(1)}, bf16[8,96,768]{2,1,0:T(8,128)(2,1)S(1)}, u32[]{:S(2)}, u32[]{:S(2)}) collective-permute-start(bf16[8,96,768]{2,1,0:T(8,128)(2,1)S(1)} %all_to_all.10.refs_0_), channel_id=1, source_target_pairs={{0,32},{32,64},{64,96},{96,128},{128,160},{160,192},{192,224},{224... | collective-permute-start | bytes 3538952 | tf_op jit(solution)/shard_map/ppermute | solution.py:345
  28.2 29.4 %collective-permute-start = (bf16[8,96,768]{2,1,0:T(8,128)(2,1)S(1)}, bf16[8,96,768]{2,1,0:T(8,128)(2,1)S(1)}, u32[]{:S(2)}, u32[]{:S(2)}) collective-permute-start(bf16[8,96,768]{2,1,0:T(8,128)(2,1)S(1)} %all_to_all.10.refs_0_), channel_id=1, source_target_pairs={{0,224},{32,0},{64,32},{96,64},{128,96},{160,128},{192,160},{224,1... | collective-permute-start | bytes 3538952 | tf_op jit(solution)/shard_map/ppermute | solution.py:345
  57.6 27.2 %collective-permute-start.3 = (bf16[8,96,768]{2,1,0:T(8,128)(2,1)S(1)}, bf16[8,96,768]{2,1,0:T(8,128)(2,1)S(1)}, u32[]{:S(2)}, u32[]{:S(2)}) collective-permute-start(bf16[8,96,768]{2,1,0:T(8,128)(2,1)S(1)} %collective-permute-done.1.refs_1_), channel_id=1, source_target_pairs={{0,32},{32,64},{64,96},{96,128},{128,160},{160,192},{192,224},{224... | collective-permute-start | bytes 3538952 | tf_op jit(solution)/shard_map/ppermute | solution.py:345
  57.6 27.2 %collective-permute-start.2 = (bf16[8,96,768]{2,1,0:T(8,128)(2,1)S(1)}, bf16[8,96,768]{2,1,0:T(8,128)(2,1)S(1)}, u32[]{:S(2)}, u32[]{:S(2)}) collective-permute-start(bf16[8,96,768]{2,1,0:T(8,128)(2,1)S(1)} %collective-permute-done.refs_0_), channel_id=1, source_target_pairs={{0,224},{32,0},{64,32},{96,64},{128,96},{160,128},{192,160},{224,1... | collective-permute-start | bytes 3538952 | tf_op jit(solution)/shard_map/ppermute | solution.py:345
  84.8 26.3 %collective-permute-start.5 = (bf16[8,96,768]{2,1,0:T(8,128)(2,1)S(1)}, bf16[8,96,768]{2,1,0:T(8,128)(2,1)S(1)}, u32[]{:S(2)}, u32[]{:S(2)}) collective-permute-start(bf16[8,96,768]{2,1,0:T(8,128)(2,1)S(1)} %collective-permute-done.3.refs_1_), channel_id=1, source_target_pairs={{0,32},{32,64},{64,96},{96,128},{128,160},{160,192},{192,224},{224... | collective-permute-start | bytes 3538952 | tf_op jit(solution)/shard_map/ppermute | solution.py:345
  84.8 26.4 %collective-permute-start.4 = (bf16[8,96,768]{2,1,0:T(8,128)(2,1)S(1)}, bf16[8,96,768]{2,1,0:T(8,128)(2,1)S(1)}, u32[]{:S(2)}, u32[]{:S(2)}) collective-permute-start(bf16[8,96,768]{2,1,0:T(8,128)(2,1)S(1)} %collective-permute-done.2.refs_0_), channel_id=1, source_target_pairs={{0,224},{32,0},{64,32},{96,64},{128,96},{160,128},{192,160},{224,1... | collective-permute-start | bytes 3538952 | tf_op jit(solution)/shard_map/ppermute | solution.py:345
  111.2 12.8 %collective-permute-start.6 = (bf16[4,96,768]{2,1,0:T(8,128)(2,1)S(1)}, bf16[4,96,768]{2,1,0:T(8,128)(2,1)S(1)}, u32[]{:S(2)}, u32[]{:S(2)}) collective-permute-start(bf16[4,96,768]{2,1,0:T(8,128)(2,1)S(1)} %slice.8), channel_id=1, source_target_pairs={{0,32},{32,64},{64,96},{96,128},{128,160},{160,192},{192,224},{224... | collective-permute-start | bytes 1769480 | tf_op jit(solution)/shard_map/ppermute | solution.py:345
  111.3 12.7 %collective-permute-start.7 = (bf16[4,96,768]{2,1,0:T(8,128)(2,1)S(1)}, bf16[4,96,768]{2,1,0:T(8,128)(2,1)S(1)}, u32[]{:S(2)}, u32[]{:S(2)}) collective-permute-start(bf16[4,96,768]{2,1,0:T(8,128)(2,1)S(1)} %slice.9), channel_id=1, source_target_pairs={{0,224},{32,0},{64,32},{96,64},{128,96},{160,128},{192,160},{224,1... | collective-permute-start | bytes 1769480 | tf_op jit(solution)/shard_map/ppermute | solution.py:345
  132.3 7.1 %collective-permute-start.8 = (bf16[208,768]{1,0:T(8,128)(2,1)S(1)}, bf16[208,768]{1,0:T(8,128)(2,1)S(1)}, u32[]{:S(2)}, u32[]{:S(2)}) collective-permute-start(bf16[208,768]{1,0:T(8,128)(2,1)S(1)} %get-tuple-element.44), channel_id=1, source_target_pairs={{0,32},{32,64},{64,96},{96,128},{128,160},{160,192},{192,224},{224... | collective-permute-start | bytes 958472 | tf_op jit(solution)/shard_map/ppermute | solution.py:345
  132.4 6.3 %collective-permute-start.9 = (bf16[192,768]{1,0:T(8,128)(2,1)S(1)}, bf16[192,768]{1,0:T(8,128)(2,1)S(1)}, u32[]{:S(2)}, u32[]{:S(2)}) collective-permute-start(bf16[192,768]{1,0:T(8,128)(2,1)S(1)} %get-tuple-element.45), channel_id=1, source_target_pairs={{0,224},{32,0},{64,32},{96,64},{128,96},{160,128},{192,160},{224,1... | collective-permute-start | bytes 884744 | tf_op jit(solution)/shard_map/ppermute | solution.py:345
  142.7 11.3 %collective-permute-start.10 = (bf16[400,768]{1,0:T(8,128)(2,1)S(1)}, bf16[400,768]{1,0:T(8,128)(2,1)S(1)}, u32[]{:S(2)}, u32[]{:S(2)}) collective-permute-start(bf16[400,768]{1,0:T(8,128)(2,1)S(1)} %get-tuple-element.46), channel_id=1, source_target_pairs={{0,32},{32,64},{64,96},{96,128},{128,160},{160,192},{192,224},{224... | collective-permute-start | bytes 1843208 | tf_op jit(solution)/shard_map/ppermute | solution.py:345
  143.5 10.4 %collective-permute-start.11 = (bf16[400,768]{1,0:T(8,128)(2,1)S(1)}, bf16[400,768]{1,0:T(8,128)(2,1)S(1)}, u32[]{:S(2)}, u32[]{:S(2)}) collective-permute-start(bf16[400,768]{1,0:T(8,128)(2,1)S(1)} %get-tuple-element.47), channel_id=1, source_target_pairs={{0,224},{32,0},{64,32},{96,64},{128,96},{160,128},{192,160},{224,1... | collective-permute-start | bytes 1843208 | tf_op jit(solution)/shard_map/ppermute | solution.py:345
  157.2 10.5 %collective-permute-start.12 = (bf16[400,768]{1,0:T(8,128)(2,1)S(1)}, bf16[400,768]{1,0:T(8,128)(2,1)S(1)}, u32[]{:S(2)}, u32[]{:S(2)}) collective-permute-start(bf16[400,768]{1,0:T(8,128)(2,1)S(1)} %get-tuple-element.48), channel_id=1, source_target_pairs={{0,32},{32,64},{64,96},{96,128},{128,160},{160,192},{192,224},{224... | collective-permute-start | bytes 1843208 | tf_op jit(solution)/shard_map/ppermute | solution.py:345
  157.8 9.9 %collective-permute-start.13 = (bf16[400,768]{1,0:T(8,128)(2,1)S(1)}, bf16[400,768]{1,0:T(8,128)(2,1)S(1)}, u32[]{:S(2)}, u32[]{:S(2)}) collective-permute-start(bf16[400,768]{1,0:T(8,128)(2,1)S(1)} %get-tuple-element.49), channel_id=1, source_target_pairs={{0,224},{32,0},{64,32},{96,64},{128,96},{160,128},{192,160},{224,1... | collective-permute-start | bytes 1843208 | tf_op jit(solution)/shard_map/ppermute | solution.py:345
  167.7 6.1 %copy-start.3 = (bf16[1,256,6144]{2,1,0:T(8,128)(2,1)S(1)}, bf16[1,256,6144]{2,1,0:T(8,128)(2,1)}, u32[]{:S(2)}) copy-start(bf16[1,256,6144]{2,1,0:T(8,128)(2,1)} %refs_4_.8) | copy-start | bytes 9437188
  170.9 10.3 %collective-permute-start.14 = (bf16[400,768]{1,0:T(8,128)(2,1)S(1)}, bf16[400,768]{1,0:T(8,128)(2,1)S(1)}, u32[]{:S(2)}, u32[]{:S(2)}) collective-permute-start(bf16[400,768]{1,0:T(8,128)(2,1)S(1)} %get-tuple-element.50), channel_id=1, source_target_pairs={{0,32},{32,64},{64,96},{96,128},{128,160},{160,192},{192,224},{224... | collective-permute-start | bytes 1843208 | tf_op jit(solution)/shard_map/ppermute | solution.py:345
  171.6 9.6 %collective-permute-start.15 = (bf16[400,768]{1,0:T(8,128)(2,1)S(1)}, bf16[400,768]{1,0:T(8,128)(2,1)S(1)}, u32[]{:S(2)}, u32[]{:S(2)}) collective-permute-start(bf16[400,768]{1,0:T(8,128)(2,1)S(1)} %get-tuple-element.51), channel_id=1, source_target_pairs={{0,224},{32,0},{64,32},{96,64},{128,96},{160,128},{192,160},{224,1... | collective-permute-start | bytes 1843208 | tf_op jit(solution)/shard_map/ppermute | solution.py:345
  184.1 23.9 %copy-start.7 = (s32[128,2]{0,1:T(2,128)S(1)}, s32[128,2]{0,1:T(2,128)}, u32[]{:S(2)}) copy-start(s32[128,2]{0,1:T(2,128)} %param.9) | copy-start | bytes 3076
  184.1 23.9 %copy-start.8 = (f32[128,2]{0,1:T(2,128)S(1)}, f32[128,2]{0,1:T(2,128)}, u32[]{:S(2)}) copy-start(f32[128,2]{0,1:T(2,128)} %param.10) | copy-start | bytes 3076
  211.2 7.2 %collective-permute-start.16 = (bf16[144,768]{1,0:T(8,128)(2,1)S(1)}, bf16[144,768]{1,0:T(8,128)(2,1)S(1)}, u32[]{:S(2)}, u32[]{:S(2)}) collective-permute-start(bf16[144,768]{1,0:T(8,128)(2,1)S(1)} %combine.1.a_ref), channel_id=1, source_target_pairs={{0,1},{1,2},{2,3},{3,0},{4,5},{5,6},{6,7},{7,4},{8,9},{9,10},{10,1... | collective-permute-start | bytes 663560 | tf_op jit(solution)/shard_map/ppermute | solution.py:345
  212.5 11.6 %collective-permute-start.17 = (bf16[144,768]{1,0:T(8,128)(2,1)S(1)}, bf16[144,768]{1,0:T(8,128)(2,1)S(1)}, u32[]{:S(2)}, u32[]{:S(2)}) collective-permute-start(bf16[144,768]{1,0:T(8,128)(2,1)S(1)} %combine.1.a_ref), channel_id=1, source_target_pairs={{0,2},{1,3},{2,0},{3,1},{4,6},{5,7},{6,4},{7,5},{8,10},{9,11},{10,... | collective-permute-start | bytes 663560 | tf_op jit(solution)/shard_map/ppermute | solution.py:345
  215.0 9.2 %collective-permute-start.18 = (bf16[144,768]{1,0:T(8,128)(2,1)S(1)}, bf16[144,768]{1,0:T(8,128)(2,1)S(1)}, u32[]{:S(2)}, u32[]{:S(2)}) collective-permute-start(bf16[144,768]{1,0:T(8,128)(2,1)S(1)} %combine.1.a_ref), channel_id=1, source_target_pairs={{0,3},{1,0},{2,1},{3,2},{4,7},{5,4},{6,5},{7,6},{8,11},{9,8},{10,9... | collective-permute-start | bytes 663560 | tf_op jit(solution)/shard_map/ppermute | solution.py:345
  (4 other events, 4.4 us)

commit v2 on v1

--- a/solution.py
+++ b/solution.py
@@ -9,6 +9,8 @@
 
 EXPERTS = 8
 CAP = 48
+WHOLE = 256
+PART = 128
 BF = jnp.bfloat16
 F32 = jnp.float32
 HIGH = lax.Precision.HIGHEST
@@ -35,36 +37,70 @@
     return ind0, ind1, count.astype(jnp.int32)
 
 
-def dispatch_kernel(ids_ref, tok_ref, og_ref, out_ref):
+def dispatch_kernel(place_ref, ids_ref, tok_ref, og_ref, out_ref):
     ind0, ind1, count = slot_masks(ids_ref[...])
     ind = ind0 + ind1
     tokens = ind.shape[1]
     slots = lax.broadcasted_iota(jnp.int32, (CAP, tokens), 0)
+    quarter = pl.ds(pl.multiple_of(WHOLE + place_ref[1] * PART, 128), PART)
+    tok, og = tok_ref[:, 0:WHOLE], og_ref[:, 0:WHOLE]
+    tok_part, og_part = tok_ref[:, quarter], og_ref[:, quarter]
     for e in range(EXPERTS):
         pick = jnp.where(count[e : e + 1, :] == slots, ind[e : e + 1, :], 0.0).astype(BF)
-        out_ref[e, 0:CAP, :] = jnp.dot(pick, tok_ref[...], preferred_element_type=F32).astype(BF)
-        out_ref[e, CAP : 2 * CAP, :] = jnp.dot(
-            pick, og_ref[...], preferred_element_type=F32
-        ).astype(BF)
-
-
-def dispatch(ids, tokens, out_grad):
-    width = tokens.shape[1]
+        column = 0
+        for source in (tok, og, tok_part, og_part):
+            width = source.shape[1]
+            out_ref[e, :, column : column + width] = jnp.dot(
+                pick, source, preferred_element_type=F32
+            ).astype(BF)
+            column += width
+
+
+def dispatch(place, ids, tokens, out_grad):
     return pl.pallas_call(
         dispatch_kernel,
-        out_shape=jax.ShapeDtypeStruct((EXPERTS, 2 * CAP, width), BF),
+        in_specs=[pl.BlockSpec(memory_space=pltpu.SMEM)]
+        + [pl.BlockSpec(memory_space=pltpu.VMEM)] * 3,
+        out_shape=jax.ShapeDtypeStruct((EXPERTS, CAP, 2 * (WHOLE + PART)), BF),
         compiler_params=pltpu.CompilerParams(vmem_limit_bytes=24 << 20),
         name="dispatch",
-    )(ids, tokens, out_grad)
-
-
-def forward_kernel(count, halves, *refs):
-    n_in = 2 if halves else count
-    ins = refs[:n_in]
-    wg_ref, wu_ref, wd_ref = refs[n_in : n_in + 3]
-    outs = refs[n_in + 3 : n_in + 3 + 2 * count]
-    acc_g, acc_u, acc_b = refs[n_in + 3 + 2 * count :]
+    )(place, ids, tokens, out_grad)
+
+
+def pieces_near(refs, e):
+    own, s_ref, p_ref, m_ref, hd_ref, hu_ref = refs[:4], *refs[4:]
+    found = [[r[0] for r in own]]
+    for i in range(4):
+        two = hd_ref[i, 0] if i < 2 else hu_ref[i - 2, 0]
+        found.append([s_ref[i, 0], p_ref[i, 0], m_ref[i, 0], two])
+    return found
+
+
+def pieces_far(refs, e):
+    s_ref, p_ref, m_ref, hd_ref, hu_ref = refs
+    late = e // (EXPERTS // 2)
+    found = []
+    for first, step in ((0, 1), (3, 1), (2, 3)):
+        i = first + step * late
+        if first == 0:
+            two = hd_ref[late, 0]
+        elif first == 3:
+            two = hu_ref[late, 0]
+        else:
+            two = jnp.where(late == 0, hd_ref[2, 0], hu_ref[2, 0])
+        found.append([s_ref[i, 0], p_ref[i, 0], m_ref[i, 0], two])
+    return found
+
+
+def forward_kernel(pieces, count, n_parts, place_ref, *refs):
+    whole = refs[:count]
+    parts = refs[count : count + n_parts]
+    rest = refs[count + n_parts :]
+    wg_ref, wu_ref, wd_ref = rest[:3]
+    outs = rest[3 : 3 + 2 * count]
+    acc_g, acc_u, acc_b, tok_ref, og_ref = rest[3 + 2 * count :]
     e = pl.program_id(0)
+    x = place_ref[1]
 
     @pl.when(e == 0)
     def _():
@@ -72,15 +108,19 @@
         acc_u[...] = jnp.zeros_like(acc_u)
         acc_b[...] = jnp.zeros_like(acc_b)
 
-    if halves:
-        blocks = [jnp.where(e < EXPERTS // 2, ins[0][0], ins[1][0])]
-    else:
-        blocks = [r[0] for r in ins]
-    tok = jnp.concatenate([b[:CAP] for b in blocks], axis=0)
-    og = jnp.concatenate([b[CAP:] for b in blocks], axis=0)
+    for i, found in enumerate(pieces(parts, e)):
+        rows = slice(i * CAP, (i + 1) * CAP)
+        tok_ref[rows, 0:WHOLE] = whole[i][0, 0, :, 0:WHOLE]
+        og_ref[rows, 0:WHOLE] = whole[i][0, 0, :, WHOLE : 2 * WHOLE]
+        for piece, offset in zip(found, (0, 3, 1, 2)):
+            there = lax.rem(x + offset, 4)
+            columns = pl.ds(pl.multiple_of(WHOLE + there * PART, 128), PART)
+            tok_ref[rows, columns] = piece[:, 0:PART]
+            og_ref[rows, columns] = piece[:, PART : 2 * PART]
+    tok = tok_ref[...]
     acc_g[...] += jnp.dot(tok, wg_ref[0], preferred_element_type=F32)
     acc_u[...] += jnp.dot(tok, wu_ref[0], preferred_element_type=F32)
-    acc_b[...] += nt(og, wd_ref[0])
+    acc_b[...] += nt(og_ref[...], wd_ref[0])
 
     @pl.when(e == EXPERTS - 1)
     def _():
@@ -102,40 +142,51 @@
             )
 
 
-def forward(blocks, halves, w_gate, w_up, w_down):
+def forward(pieces, dists, place, whole, parts, w_gate, w_up, w_down):
     hidden = w_gate.shape[2]
-    width = blocks[0].shape[2]
-    count = 1 if halves else len(blocks)
-    shape = (1, 2 * CAP, width)
-    if halves:
-        last = EXPERTS // 2 - 1
-        in_specs = [
-            pl.BlockSpec(shape, lambda e: (jnp.minimum(e, last), 0, 0)),
-            pl.BlockSpec(shape, lambda e: (jnp.maximum(e - last - 1, 0), 0, 0)),
-        ]
-    else:
-        in_specs = [pl.BlockSpec(shape, lambda e: (e, 0, 0)) for _ in blocks]
+    width = w_gate.shape[1] // EXPERTS
+    count = len(dists)
+    n_dp = whole.shape[0]
+
+    def whole_spec(dist):
+        return pl.BlockSpec(
+            (1, 1, CAP, 2 * WHOLE), lambda e, at: (lax.rem(at[0] + dist, n_dp), e, 0, 0)
+        )
+
+    def part_spec(a):
+        if a.ndim == 3:
+            return pl.BlockSpec((1, CAP, 2 * PART), lambda e, at: (e, 0, 0))
+        length = a.shape[1]
+        return pl.BlockSpec(
+            (a.shape[0], 1, CAP, 2 * PART), lambda e, at: (0, lax.rem(e, length), 0, 0)
+        )
+
+    in_specs = [whole_spec(dist % n_dp) for dist in dists] + [part_spec(a) for a in parts]
     in_specs += [
-        pl.BlockSpec((1, width, hidden), lambda e: (0, e, 0)),
-        pl.BlockSpec((1, width, hidden), lambda e: (0, e, 0)),
-        pl.BlockSpec((1, hidden, width), lambda e: (0, 0, e)),
+        pl.BlockSpec((1, width, hidden), lambda e, at: (0, e, 0)),
+        pl.BlockSpec((1, width, hidden), lambda e, at: (0, e, 0)),
+        pl.BlockSpec((1, hidden, width), lambda e, at: (0, 0, e)),
     ]
     rows = count * CAP
     outs = pl.pallas_call(
-        functools.partial(forward_kernel, count, halves),
-        grid=(EXPERTS,),
-        in_specs=in_specs,
-        out_specs=[
-            pl.BlockSpec((CAP, 2 * hidden), lambda e: (0, 0)),
-            pl.BlockSpec((16, 128), lambda e: (0, 0)),
-        ]
-        * count,
+        functools.partial(forward_kernel, pieces, count, len(parts)),
+        grid_spec=pltpu.PrefetchScalarGridSpec(
+            num_scalar_prefetch=1,
+            grid=(EXPERTS,),
+            in_specs=in_specs,
+            out_specs=[
+                pl.BlockSpec((CAP, 2 * hidden), lambda e, at: (0, 0)),
+                pl.BlockSpec((16, 128), lambda e, at: (0, 0)),
+            ]
+            * count,
+            scratch_shapes=[pltpu.VMEM((rows, hidden), F32)] * 3
+            + [pltpu.VMEM((rows, width), BF)] * 2,
+        ),
         out_shape=[
             jax.ShapeDtypeStruct((CAP, 2 * hidden), BF),
             jax.ShapeDtypeStruct((16, 128), F32),
         ]
         * count,
-        scratch_shapes=[pltpu.VMEM((rows, hidden), F32)] * 3,
         compiler_params=pltpu.CompilerParams(vmem_limit_bytes=24 << 20),
         cost_estimate=pl.CostEstimate(
             flops=6 * 256 * EXPERTS * width * hidden,
@@ -143,7 +194,7 @@
             transcendentals=0,
         ),
         name="forward",
-    )(*blocks, w_gate, w_up, w_down)
+    )(place, *([whole] * count), *parts, w_gate, w_up, w_down)
     return [(outs[2 * i], outs[2 * i + 1]) for i in range(count)]
 
 
@@ -345,21 +396,40 @@
     return lax.ppermute(a, axis, [(i, (i + by) % n) for i in range(n)])
 
 
+def spread(stacked, split):
+    plus, minus = shift(stacked, "tensor", 1), shift(stacked, "tensor", -1)
+    ahead, behind = shift(plus[:split], "tensor", 1), shift(minus[split:], "tensor", -1)
+    return stacked, plus, minus, ahead, behind
+
+
 def per_device(tokens, out_grad, expert_ids, combine_weights, w_gate, w_up, w_down):
     ids = expert_ids.T
     weights = combine_weights.T
     half = EXPERTS // 2
-    send = dispatch(ids, tokens, out_grad)
+    place = jnp.stack([lax.axis_index("dp"), lax.axis_index("tensor")]).astype(jnp.int32)
+    send = dispatch(place, ids, tokens, out_grad)
     own = lax.all_to_all(send, "expert", split_axis=0, concat_axis=0)
-    up, down = own, own
-    grads = {}
-    blocks = {0: [own]}
+    whole, part = own[:, :, : 2 * WHOLE], own[:, :, 2 * WHOLE :]
+
+    up, down = part, part
+    behind, ahead = {}, {}
     for dist in range(1, 4):
         up, down = shift(up, "dp", 1), shift(down, "dp", -1)
-        blocks[dist] = [down, up]
-    blocks[4] = [shift(up[:half], "dp", 1), shift(down[half:], "dp", -1)]
-    for dist in range(5):
-        grads[dist] = forward(blocks[dist], dist == 4, w_gate, w_up, w_down)
+        behind[dist], ahead[dist] = up, down
+    low, high = shift(up[:half], "dp", 1), shift(down[half:], "dp", -1)
+    whole = lax.optimization_barrier((whole, behind[1], ahead[1]))[0]
+    whole = lax.all_gather(whole, "dp", axis=0)
+
+    near = [part] + [shift(part, "tensor", by) for by in (1, -1, 2)]
+    stacked = jnp.concatenate([ahead[1], ahead[2], behind[1], behind[2]], axis=0)
+    near += [a.reshape(-1, EXPERTS, *a.shape[1:]) for a in spread(stacked, 2 * EXPERTS)]
+    stacked = jnp.concatenate([ahead[3], low, behind[3], high], axis=0)
+    far = [a.reshape(-1, half, *a.shape[1:]) for a in spread(stacked, EXPERTS + half)]
+
+    outs = forward(pieces_near, (0, 1, 2, -1, -2), place, whole, near, w_gate, w_up, w_down)
+    outs += forward(pieces_far, (3, -3, 4), place, whole, far, w_gate, w_up, w_down)
+    grads = {0: [outs[0]], 1: [outs[1], outs[3]], 2: [outs[2], outs[4]]}
+    grads.update({3: [outs[5], outs[6]], 4: [outs[7]]})
     received = ()
     for dist in range(4, 0, -1):
         small = [a for pair in grads[dist] for a in pair]

time: 225 us -> 223 us (level)
  waiting for transfers between devices: 105 us -> 63.4 us
  local copies, waits for them, and re-layouts: 4.51 us -> 23.1 us
  between operations: 0.79 us -> 14.3 us
  starting transfers between devices: 29.9 us -> 42.9 us
  Pallas kernels: 38.1 us -> 33.7 us
    ppermute x19 -> x30, waiting for transfers between devices: 105 us -> 60 us  [shift(): return lax.ppermute(a, axis, [(i, (i + by) % n) for i in range(n)])]
    unnamed x18 -> x50, local copies, waits for them, and re-layouts: 4.44 us -> 19.4 us
    ppermute x19 -> x30, starting transfers between devices: 29.9 us -> 42.9 us  [shift(): return lax.ppermute(a, axis, [(i, (i + by) % n) for i in range(n)])]
    all_to_all x1, blocking collectives: 22.7 us -> 16.1 us  [per_device(): own = lax.all_to_all(send, 'expert', split_axis=0, concat_axis=0)]
    all_to_all x1, blocking collectives: 23.9 us -> 28.6 us  [per_device(): rows = lax.all_to_all(rows, 'expert', split_axis=0, concat_axis=0)]
    pallas_call x6 -> x3, Pallas kernels: 18.6 us -> 14.2 us  [the longest x2 13.1 us: forward(): pl.pallas_call(functools.partial(forward_kernel, pieces, count, len(parts...]
    all_gather x0 -> x1, waiting for transfers between devices: none -> 3.41 us  [per_device(): whole = lax.all_gather(whole, 'dp', axis=0)]
    slice x2 -> x8, local copies, waits for them, and re-layouts: 0.08 us -> 2.94 us  [the longest x2 1.04 us: spread(): plus[:split]]
  transfers between devices with their start and end apart: 19 -> 31, of which waited for: 10 -> 16; matrix products, arithmetic and copies ran while one was open for 0% -> 3% of each run, Pallas kernels for 6% -> 9%
where the time goes in v2:
time: 223 us; the launch traced here: 222 us
  waiting for transfers between devices  63.4 us (28%)
  blocking collectives  44.7 us (20%)
  starting transfers between devices  42.9 us (19%)
  Pallas kernels  33.7 us (15%)
  local copies, waits for them, and re-layouts  23.1 us (10%)
  between operations  14.3 us (6%)
    ppermute x30, waiting for transfers between devices, shift(): return lax.ppermute(a, axis, [(i, (i + by) % n) for i in range(n)])  60 us
    ppermute x30, starting transfers between devices, shift(): return lax.ppermute(a, axis, [(i, (i + by) % n) for i in range(n)])  42.9 us
    all_to_all x1, blocking collectives, per_device(): rows = lax.all_to_all(rows, 'expert', split_axis=0, concat_axis=0)  28.6 us
    unnamed x50, local copies, waits for them, and re-layouts  19.4 us
    all_to_all x1, blocking collectives, per_device(): own = lax.all_to_all(send, 'expert', split_axis=0, concat_axis=0)  16.1 us
    pallas_call x5, Pallas kernels, backward(): pl.pallas_call(functools.partial(backward_kernel, dist), grid=(EXPERTS,),...  15.5 us
    pallas_call x2, Pallas kernels, forward(): pl.pallas_call(functools.partial(forward_kernel, pieces, count, len(parts...  13.1 us
  transfers between devices with their start and end apart: 31, of which 16 were waited for; matrix products, arithmetic and copies ran while one was open for 3% of the time, Pallas kernels for 9%

profile of v2, /device:TPU:1, one launch (start us, length us, event | category | flops | bytes accessed | tf_op | source)
XLA Modules:
  0.0 222.1 jit_solution(18127459390870530020)
XLA Ops:
  10.9 16.1 %all_to_all.10 = bf16[8,48,768]{2,1,0:T(8,128)(2,1)S(1)} all-to-all(bf16[8,48,768]{2,1,0:T(8,128)(2,1)S(1)} %dispatch.1), channel_id=1, replica_groups=mesh['dp'=8,'expert'=8,'tensor'=4] {'expert'}, dimensions={0} | all-to-all | bytes 1179648 | tf_op jit(solution)/shard_map/all_to_all | solution.py:411
  28.8 4.0 %collective-permute-start.1 = (bf16[8,48,256]{2,1,0:T(8,128)(2,1)S(1)}, bf16[8,48,256]{2,1,0:T(8,128)(2,1)}, u32[]{:S(2)}, u32[]{:S(2)}) collective-permute-start(bf16[8,48,256]{2,1,0:T(8,128)(2,1)S(1)} %slice.33.refs_5_), channel_id=1, source_target_pairs={{0,224},{32,0},{64,32},{96,64},{128,96},{160,128},{192,160},{224,1... | collective-permute-start | bytes 589832 | tf_op jit(solution)/shard_map/ppermute | solution.py:396
  33.6 3.6 %collective-permute-done = bf16[8,48,256]{2,1,0:T(8,128)(2,1)S(1)} collective-permute-done((bf16[8,48,256]{2,1,0:T(8,128)(2,1)S(1)}, bf16[8,48,256]{2,1,0:T(8,128)(2,1)S(1)}, u32[]{:S(2)}, u32[]{:S(2)}) %collective-permute-start) | collective-permute-done | bytes 196640 | tf_op jit(solution)/shard_map/ppermute | solution.py:396
  40.0 3.6 %collective-permute-done.6 = bf16[8,48,256]{2,1,0:T(8,128)(2,1)S(1)} collective-permute-done((bf16[8,48,256]{2,1,0:T(8,128)(2,1)S(1)}, bf16[8,48,256]{2,1,0:T(8,128)(2,1)S(1)}, u32[]{:S(2)}, u32[]{:S(2)}) %collective-permute-start.6) | collective-permute-done | bytes 196640 | tf_op jit(solution)/shard_map/ppermute | solution.py:396
  46.3 3.0 %collective-permute-done.12 = bf16[8,48,256]{2,1,0:T(8,128)(2,1)S(1)} collective-permute-done((bf16[8,48,256]{2,1,0:T(8,128)(2,1)S(1)}, bf16[8,48,256]{2,1,0:T(8,128)(2,1)S(1)}, u32[]{:S(2)}, u32[]{:S(2)}) %collective-permute-start.12) | collective-permute-done | bytes 196640 | tf_op jit(solution)/shard_map/ppermute | solution.py:396
  51.8 3.6 %collective-permute-start.14 = (bf16[4,48,256]{2,1,0:T(8,128)(2,1)S(1)}, bf16[4,48,256]{2,1,0:T(8,128)(2,1)S(1)}, u32[]{:S(2)}, u32[]{:S(2)}) collective-permute-start(bf16[4,48,256]{2,1,0:T(8,128)(2,1)S(1)} %slice.37), channel_id=1, source_target_pairs={{0,224},{32,0},{64,32},{96,64},{128,96},{160,128},{192,160},{224,1... | collective-permute-start | bytes 294920 | tf_op jit(solution)/shard_map/ppermute | solution.py:396
  64.3 5.4 %collective-permute-done.15 = bf16[24,48,256]{2,1,0:T(8,128)(2,1)S(1)} collective-permute-done((bf16[24,48,256]{2,1,0:T(8,128)(2,1)S(1)}, bf16[24,48,256]{2,1,0:T(8,128)(2,1)S(1)}, u32[]{:S(2)}, u32[]{:S(2)}) %collective-permute-start.15) | collective-permute-done | bytes 589856 | tf_op jit(solution)/shard_map/ppermute | solution.py:396
  80.6 3.4 %all-gather.3.cloned.1.call-done = bf16[64,48,512]{2,1,0:T(8,128)(2,1)} async-done(((bf16[8,48,512]{2,1,0:T(8,128)(2,1)}), bf16[64,48,512]{2,1,0:T(8,128)(2,1)}) %all-gather.3.cloned.1.call-update) | async-done | bytes 3145744 | tf_op jit(solution)/shard_map/all_gather | solution.py:421
  94.8 5.3 %forward.3 = (bf16[48,512]{1,0:T(8,128)(2,1)S(1)}, f32[16,128]{1,0:T(8,128)S(1)}, bf16[48,512]{1,0:T(8,128)(2,1)S(1)}, f32[16,128]{1,0:T(8,128)S(1)}, bf16[48,51...) custom-call(s32[2]{0:T(128)S(1)} %pad_add_fusion.place_ref, bf16[8,8,48,512]{3,2,1,0:T(8,128)(2,1)S(1)} %bitcast.16, ...), custom_call_target="tpu_custom_call" | custom-call | flops 2415919104 | bytes 9437184 | tf_op jit(solution)/shard_map/forward/pallas_call | solution.py:171
  100.1 2.9 %backward.5 = (bf16[208,768]{1,0:T(8,128)(2,1)S(1)}, bf16[192,768]{1,0:T(8,128)(2,1)S(1)}) custom-call(bf16[48,512]{1,0:T(8,128)(2,1)S(1)} %get-tuple-element.44.refs_0_, f32[16,128]{1,0:T(8,128)S(1)} %get-tuple-element.45.refs_1_, bf16[1,6144,256]{2,1,0:T(8,128)(2,1)S(1)} %copy-done.2, bf16[1,6144,256]{2,1,0:T(8,128)(2,1)S(1)} %copy-done.4), custom_call_target="tpu_custom_call" | custom-call | flops 1610612736 | bytes 6291456 | tf_op jit(solution)/shard_map/backward/pallas_call | solution.py:312
  110.6 2.7 %collective-permute-start.10 = (bf16[16,48,256]{2,1,0:T(8,128)(2,1)S(1)}, bf16[16,48,256]{2,1,0:T(8,128)(2,1)S(1)}, u32[]{:S(2)}, u32[]{:S(2)}) collective-permute-start(bf16[16,48,256]{2,1,0:T(8,128)(2,1)S(1)} %slice.35), channel_id=1, source_target_pairs={{0,3},{1,0},{2,1},{3,2},{4,7},{5,4},{6,5},{7,6},{8,11},{9,8},{10,9... | collective-permute-start | bytes 1179656 | tf_op jit(solution)/shard_map/ppermute | solution.py:396
  113.3 3.2 %backward.6 = (bf16[400,768]{1,0:T(8,128)(2,1)S(1)}, bf16[400,768]{1,0:T(8,128)(2,1)S(1)}) custom-call(bf16[48,512]{1,0:T(8,128)(2,1)S(1)} %get-tuple-element.40.refs_0_, f32[16,128]{1,0:T(8,128)S(1)} %get-tuple-element.41.refs_1_, bf16[48,512]{1,0:T(8,128)(2,1)S(1)} %get-tuple-element.42.refs_2_, f32[16,128]{1,0:T(8,128)S(1)} %get-tuple-element.43.refs_3_, ...), custom_call_target="tpu_custom_call" | custom-call | flops 1610612736 | bytes 6291456 | tf_op jit(solution)/shard_map/backward/pallas_call | solution.py:312
  119.7 7.7 %collective-permute-done.4.refs_8_ = bf16[8,48,256]{2,1,0:T(8,128)(2,1)S(1)} collective-permute-done((bf16[8,48,256]{2,1,0:T(8,128)(2,1)S(1)}, bf16[8,48,256]{2,1,0:T(8,128)(2,1)S(1)}, u32[]{:S(2)}, u32[]{:S(2)}) %collective-permute-start.4) | collective-permute-done | bytes 196640 | tf_op jit(solution)/shard_map/ppermute | solution.py:396
  127.4 7.8 %forward.2 = (bf16[48,512]{1,0:T(8,128)(2,1)S(1)}, f32[16,128]{1,0:T(8,128)S(1)}, bf16[48,512]{1,0:T(8,128)(2,1)S(1)}, f32[16,128]{1,0:T(8,128)S(1)}, bf16[48,51...) custom-call(s32[2]{0:T(128)S(1)} %pad_add_fusion.place_ref, ...), custom_call_target="tpu_custom_call" | custom-call | flops 2415919104 | bytes 9437184 | tf_op jit(solution)/shard_map/forward/pallas_call | solution.py:171
  135.3 3.3 %backward.7 = (bf16[400,768]{1,0:T(8,128)(2,1)S(1)}, bf16[400,768]{1,0:T(8,128)(2,1)S(1)}) custom-call(bf16[48,512]{1,0:T(8,128)(2,1)S(1)} %get-tuple-element.36.refs_0_, f32[16,128]{1,0:T(8,128)S(1)} %get-tuple-element.37.refs_1_, bf16[48,512]{1,0:T(8,128)(2,1)S(1)} %get-tuple-element.38.refs_2_, f32[16,128]{1,0:T(8,128)S(1)} %get-tuple-element.39.refs_3_, ...), custom_call_target="tpu_custom_call" | custom-call | flops 1610612736 | bytes 6291456 | tf_op jit(solution)/shard_map/backward/pallas_call | solution.py:312
  141.3 7.5 %collective-permute-done.23.refs_4_ = bf16[400,768]{1,0:T(8,128)(2,1)S(1)} collective-permute-done((bf16[400,768]{1,0:T(8,128)(2,1)S(1)}, bf16[400,768]{1,0:T(8,128)(2,1)S(1)}, u32[]{:S(2)}, u32[]{:S(2)}) %collective-permute-start.23) | collective-permute-done | bytes 614432 | tf_op jit(solution)/shard_map/ppermute | solution.py:396
  148.9 3.3 %backward.8 = (bf16[400,768]{1,0:T(8,128)(2,1)S(1)}, bf16[400,768]{1,0:T(8,128)(2,1)S(1)}) custom-call(bf16[48,512]{1,0:T(8,128)(2,1)S(1)} %get-tuple-element.32.refs_0_, f32[16,128]{1,0:T(8,128)S(1)} %get-tuple-element.33.refs_1_, bf16[48,512]{1,0:T(8,128)(2,1)S(1)} %get-tuple-element.34.refs_2_, f32[16,128]{1,0:T(8,128)S(1)} %get-tuple-element.35.refs_3_, ...), custom_call_target="tpu_custom_call" | custom-call | flops 1610612736 | bytes 6291456 | tf_op jit(solution)/shard_map/backward/pallas_call | solution.py:312
  152.2 3.0 %collective-permute-start.26 = (bf16[400,768]{1,0:T(8,128)(2,1)S(1)}, bf16[400,768]{1,0:T(8,128)(2,1)S(1)}, u32[]{:S(2)}, u32[]{:S(2)}) collective-permute-start(bf16[400,768]{1,0:T(8,128)(2,1)S(1)} %get-tuple-element.53), channel_id=1, source_target_pairs={{0,224},{32,0},{64,32},{96,64},{128,96},{160,128},{192,160},{224,1... | collective-permute-start | bytes 1843208 | tf_op jit(solution)/shard_map/ppermute | solution.py:396
  155.2 11.0 %collective-permute-done.25.refs_2_ = bf16[400,768]{1,0:T(8,128)(2,1)S(1)} collective-permute-done((bf16[400,768]{1,0:T(8,128)(2,1)S(1)}, bf16[400,768]{1,0:T(8,128)(2,1)S(1)}, u32[]{:S(2)}, u32[]{:S(2)}) %collective-permute-start.25) | collective-permute-done | bytes 614432 | tf_op jit(solution)/shard_map/ppermute | solution.py:396
  167.6 2.8 %backward.9 = bf16[8,64,768]{2,1,0:T(8,128)(2,1)S(1)} custom-call(bf16[48,512]{1,0:T(8,128)(2,1)S(1)} %get-tuple-element.30.refs_0_, f32[16,128]{1,0:T(8,128)S(1)} %get-tuple-element.31.refs_1_, bf16[400,768]{1,0:T(8,128)(2,1)S(1)} %collective-permute-done.25.refs_2_, bf16[400,768]{1,0:T(8,128)(2,1)S(1)} %collective-permute-done.26.refs_3_, ...), custom_call_target="tpu_custom_call" | custom-call | flops 1610612736 | bytes 6291456 | tf_op jit(solution)/shard_map/backward/pallas_call | solution.py:312
  170.4 28.6 %all_to_all.11.rows_ref = bf16[8,64,768]{2,1,0:T(8,128)(2,1)S(1)} all-to-all(bf16[8,64,768]{2,1,0:T(8,128)(2,1)S(1)} %backward.9), channel_id=1, replica_groups=mesh['dp'=8,'expert'=8,'tensor'=4] {'expert'}, dimensions={0} | all-to-all | bytes 1572864 | tf_op jit(solution)/shard_map/all_to_all | solution.py:439
  199.0 3.2 %combine.1.a_ref = bf16[144,768]{1,0:T(8,128)(2,1)S(1)} custom-call(s32[2,128]{1,0:T(2,128)S(1)} %bitcast.32, f32[2,128]{1,0:T(2,128)S(1)} %bitcast.33, bf16[8,64,768]{2,1,0:T(8,128)(2,1)S(1)} %all_to_all.11.rows_ref), custom_call_target="tpu_custom_call" | custom-call | tf_op jit(solution)/shard_map/combine/pallas_call | solution.py:362
  204.9 4.9 %collective-permute-done.27.b_ref = bf16[144,768]{1,0:T(8,128)(2,1)S(1)} collective-permute-done((bf16[144,768]{1,0:T(8,128)(2,1)S(1)}, bf16[144,768]{1,0:T(8,128)(2,1)S(1)}, u32[]{:S(2)}, u32[]{:S(2)}) %collective-permute-start.27) | collective-permute-done | bytes 221216 | tf_op jit(solution)/shard_map/ppermute | solution.py:396
  209.8 3.8 %collective-permute-done.28.c_ref = bf16[144,768]{1,0:T(8,128)(2,1)S(1)} collective-permute-done((bf16[144,768]{1,0:T(8,128)(2,1)S(1)}, bf16[144,768]{1,0:T(8,128)(2,1)S(1)}, u32[]{:S(2)}, u32[]{:S(2)}) %collective-permute-start.28) | collective-permute-done | bytes 221216 | tf_op jit(solution)/shard_map/ppermute | solution.py:396
  (112 shorter events, 63.8 us)
Async XLA Ops:
  7.2 76.8 %all-gather.3.cloned.1.call-start = ((), (), s32[]{:S(2)}) async-start(), calls=%async_computation.2 | async-start | bytes 3538944 | tf_op jit(solution)/shard_map/all_gather | solution.py:421
  27.1 10.2 %collective-permute-start = (bf16[8,48,256]{2,1,0:T(8,128)(2,1)S(1)}, bf16[8,48,256]{2,1,0:T(8,128)(2,1)S(1)}, u32[]{:S(2)}, u32[]{:S(2)}) collective-permute-start(bf16[8,48,256]{2,1,0:T(8,128)(2,1)S(1)} %slice.33.refs_5_), channel_id=1, source_target_pairs={{0,32},{32,64},{64,96},{96,128},{128,160},{160,192},{192,224},{224... | collective-permute-start | bytes 589832 | tf_op jit(solution)/shard_map/ppermute | solution.py:396
  28.8 8.5 %collective-permute-start.1 = (bf16[8,48,256]{2,1,0:T(8,128)(2,1)S(1)}, bf16[8,48,256]{2,1,0:T(8,128)(2,1)}, u32[]{:S(2)}, u32[]{:S(2)}) collective-permute-start(bf16[8,48,256]{2,1,0:T(8,128)(2,1)S(1)} %slice.33.refs_5_), channel_id=1, source_target_pairs={{0,224},{32,0},{64,32},{96,64},{128,96},{160,128},{192,160},{224,1... | collective-permute-start | bytes 589832 | tf_op jit(solution)/shard_map/ppermute | solution.py:396
  43.7 8.2 %collective-permute-start.11 = (bf16[8,48,256]{2,1,0:T(8,128)(2,1)S(1)}, bf16[8,48,256]{2,1,0:T(8,128)(2,1)S(1)}, u32[]{:S(2)}, u32[]{:S(2)}) collective-permute-start(bf16[8,48,256]{2,1,0:T(8,128)(2,1)S(1)} %collective-permute-done.5), channel_id=1, source_target_pairs={{0,224},{32,0},{64,32},{96,64},{128,96},{160,128},{192,160},{224,1... | collective-permute-start | bytes 589832 | tf_op jit(solution)/shard_map/ppermute | solution.py:396
  59.2 10.5 %collective-permute-start.15 = (bf16[24,48,256]{2,1,0:T(8,128)(2,1)S(1)}, bf16[24,48,256]{2,1,0:T(8,128)(2,1)S(1)}, u32[]{:S(2)}, u32[]{:S(2)}) collective-permute-start(bf16[24,48,256]{2,1,0:T(8,128)(2,1)S(1)} %constant_dynamic-update-slice_fusion.4), channel_id=1, source_target_pairs={{0,1},{1,2},{2,3},{3,0},{4,5},{5,6},{6,7},{7,4},{8,9},{9,10},{10,1... | collective-permute-start | bytes 1769480 | tf_op jit(solution)/shard_map/ppermute | solution.py:396
  60.4 10.2 %collective-permute-start.16 = (bf16[24,48,256]{2,1,0:T(8,128)(2,1)S(1)}, bf16[24,48,256]{2,1,0:T(8,128)(2,1)S(1)}, u32[]{:S(2)}, u32[]{:S(2)}) collective-permute-start(bf16[24,48,256]{2,1,0:T(8,128)(2,1)S(1)} %constant_dynamic-update-slice_fusion.4), channel_id=1, source_target_pairs={{0,3},{1,0},{2,1},{3,2},{4,7},{5,4},{6,5},{7,6},{8,11},{9,8},{10,9... | collective-permute-start | bytes 1769480 | tf_op jit(solution)/shard_map/ppermute | solution.py:396
  70.6 8.6 %collective-permute-start.17 = (bf16[12,48,256]{2,1,0:T(8,128)(2,1)S(1)}, bf16[12,48,256]{2,1,0:T(8,128)(2,1)S(1)}, u32[]{:S(2)}, u32[]{:S(2)}) collective-permute-start(bf16[12,48,256]{2,1,0:T(8,128)(2,1)S(1)} %slice.38), channel_id=1, source_target_pairs={{0,1},{1,2},{2,3},{3,0},{4,5},{5,6},{6,7},{7,4},{8,9},{9,10},{10,1... | collective-permute-start | bytes 884744 | tf_op jit(solution)/shard_map/ppermute | solution.py:396
  71.4 8.4 %collective-permute-start.18 = (bf16[12,48,256]{2,1,0:T(8,128)(2,1)S(1)}, bf16[12,48,256]{2,1,0:T(8,128)(2,1)S(1)}, u32[]{:S(2)}, u32[]{:S(2)}) collective-permute-start(bf16[12,48,256]{2,1,0:T(8,128)(2,1)S(1)} %slice.39), channel_id=1, source_target_pairs={{0,3},{1,0},{2,1},{3,2},{4,7},{5,4},{6,5},{7,6},{8,11},{9,8},{10,9... | collective-permute-start | bytes 884744 | tf_op jit(solution)/shard_map/ppermute | solution.py:396
  75.5 31.5 %collective-permute-start.7 = (bf16[32,48,256]{2,1,0:T(8,128)(2,1)}, bf16[32,48,256]{2,1,0:T(8,128)(2,1)}, u32[]{:S(2)}, u32[]{:S(2)}) collective-permute-start(bf16[32,48,256]{2,1,0:T(8,128)(2,1)} %constant_dynamic-update-slice_fusion), channel_id=1, source_target_pairs={{0,1},{1,2},{2,3},{3,0},{4,5},{5,6},{6,7},{7,4},{8,9},{9,10},{10,1... | collective-permute-start | bytes 2359304 | tf_op jit(solution)/shard_map/ppermute | solution.py:396
  75.5 34.0 %collective-permute-start.8 = (bf16[32,48,256]{2,1,0:T(8,128)(2,1)}, bf16[32,48,256]{2,1,0:T(8,128)(2,1)}, u32[]{:S(2)}, u32[]{:S(2)}) collective-permute-start(bf16[32,48,256]{2,1,0:T(8,128)(2,1)} %constant_dynamic-update-slice_fusion), channel_id=1, source_target_pairs={{0,3},{1,0},{2,1},{3,2},{4,7},{5,4},{6,5},{7,6},{8,11},{9,8},{10,9... | collective-permute-start | bytes 2359304 | tf_op jit(solution)/shard_map/ppermute | solution.py:396
  103.0 10.3 %collective-permute-start.19 = (bf16[208,768]{1,0:T(8,128)(2,1)S(1)}, bf16[208,768]{1,0:T(8,128)(2,1)S(1)}, u32[]{:S(2)}, u32[]{:S(2)}) collective-permute-start(bf16[208,768]{1,0:T(8,128)(2,1)S(1)} %get-tuple-element.46), channel_id=1, source_target_pairs={{0,32},{32,64},{64,96},{96,128},{128,160},{160,192},{192,224},{224... | collective-permute-start | bytes 958472 | tf_op jit(solution)/shard_map/ppermute | solution.py:396
  105.8 12.1 %collective-permute-start.2 = (bf16[8,48,256]{2,1,0:T(8,128)(2,1)S(1)}, bf16[8,48,256]{2,1,0:T(8,128)(2,1)S(1)}, u32[]{:S(2)}, u32[]{:S(2)}) collective-permute-start(bf16[8,48,256]{2,1,0:T(8,128)(2,1)S(1)} %slice.33.refs_5_), channel_id=1, source_target_pairs={{0,1},{1,2},{2,3},{3,0},{4,5},{5,6},{6,7},{7,4},{8,9},{9,10},{10,1... | collective-permute-start | bytes 589832 | tf_op jit(solution)/shard_map/ppermute | solution.py:396
  107.0 12.3 %collective-permute-start.3 = (bf16[8,48,256]{2,1,0:T(8,128)(2,1)S(1)}, bf16[8,48,256]{2,1,0:T(8,128)(2,1)S(1)}, u32[]{:S(2)}, u32[]{:S(2)}) collective-permute-start(bf16[8,48,256]{2,1,0:T(8,128)(2,1)S(1)} %slice.33.refs_5_), channel_id=1, source_target_pairs={{0,3},{1,0},{2,1},{3,2},{4,7},{5,4},{6,5},{7,6},{8,11},{9,8},{10,9... | collective-permute-start | bytes 589832 | tf_op jit(solution)/shard_map/ppermute | solution.py:396
  109.5 17.9 %collective-permute-start.9 = (bf16[16,48,256]{2,1,0:T(8,128)(2,1)S(1)}, bf16[16,48,256]{2,1,0:T(8,128)(2,1)S(1)}, u32[]{:S(2)}, u32[]{:S(2)}) collective-permute-start(bf16[16,48,256]{2,1,0:T(8,128)(2,1)S(1)} %slice.34), channel_id=1, source_target_pairs={{0,1},{1,2},{2,3},{3,0},{4,5},{5,6},{6,7},{7,4},{8,9},{9,10},{10,1... | collective-permute-start | bytes 1179656 | tf_op jit(solution)/shard_map/ppermute | solution.py:396
  110.6 16.8 %collective-permute-start.10 = (bf16[16,48,256]{2,1,0:T(8,128)(2,1)S(1)}, bf16[16,48,256]{2,1,0:T(8,128)(2,1)S(1)}, u32[]{:S(2)}, u32[]{:S(2)}) collective-permute-start(bf16[16,48,256]{2,1,0:T(8,128)(2,1)S(1)} %slice.35), channel_id=1, source_target_pairs={{0,3},{1,0},{2,1},{3,2},{4,7},{5,4},{6,5},{7,6},{8,11},{9,8},{10,9... | collective-permute-start | bytes 1179656 | tf_op jit(solution)/shard_map/ppermute | solution.py:396
  116.6 18.7 %collective-permute-start.21 = (bf16[400,768]{1,0:T(8,128)(2,1)S(1)}, bf16[400,768]{1,0:T(8,128)(2,1)S(1)}, u32[]{:S(2)}, u32[]{:S(2)}) collective-permute-start(bf16[400,768]{1,0:T(8,128)(2,1)S(1)} %get-tuple-element.48), channel_id=1, source_target_pairs={{0,32},{32,64},{64,96},{96,128},{128,160},{160,192},{192,224},{224... | collective-permute-start | bytes 1843208 | tf_op jit(solution)/shard_map/ppermute | solution.py:396
  117.9 17.4 %collective-permute-start.22 = (bf16[400,768]{1,0:T(8,128)(2,1)S(1)}, bf16[400,768]{1,0:T(8,128)(2,1)S(1)}, u32[]{:S(2)}, u32[]{:S(2)}) collective-permute-start(bf16[400,768]{1,0:T(8,128)(2,1)S(1)} %get-tuple-element.49), channel_id=1, source_target_pairs={{0,224},{32,0},{64,32},{96,64},{128,96},{160,128},{192,160},{224,1... | collective-permute-start | bytes 1843208 | tf_op jit(solution)/shard_map/ppermute | solution.py:396
  119.3 8.1 %collective-permute-start.4 = (bf16[8,48,256]{2,1,0:T(8,128)(2,1)S(1)}, bf16[8,48,256]{2,1,0:T(8,128)(2,1)S(1)}, u32[]{:S(2)}, u32[]{:S(2)}) collective-permute-start(bf16[8,48,256]{2,1,0:T(8,128)(2,1)S(1)} %slice.33.refs_5_), channel_id=1, source_target_pairs={{0,2},{1,3},{2,0},{3,1},{4,6},{5,7},{6,4},{7,5},{8,10},{9,11},{10,... | collective-permute-start | bytes 589832 | tf_op jit(solution)/shard_map/ppermute | solution.py:396
  138.6 10.3 %collective-permute-start.23 = (bf16[400,768]{1,0:T(8,128)(2,1)S(1)}, bf16[400,768]{1,0:T(8,128)(2,1)S(1)}, u32[]{:S(2)}, u32[]{:S(2)}) collective-permute-start(bf16[400,768]{1,0:T(8,128)(2,1)S(1)} %get-tuple-element.50), channel_id=1, source_target_pairs={{0,32},{32,64},{64,96},{96,128},{128,160},{160,192},{192,224},{224... | collective-permute-start | bytes 1843208 | tf_op jit(solution)/shard_map/ppermute | solution.py:396
  138.8 10.0 %collective-permute-start.24 = (bf16[400,768]{1,0:T(8,128)(2,1)S(1)}, bf16[400,768]{1,0:T(8,128)(2,1)S(1)}, u32[]{:S(2)}, u32[]{:S(2)}) collective-permute-start(bf16[400,768]{1,0:T(8,128)(2,1)S(1)} %get-tuple-element.51), channel_id=1, source_target_pairs={{0,224},{32,0},{64,32},{96,64},{128,96},{160,128},{192,160},{224,1... | collective-permute-start | bytes 1843208 | tf_op jit(solution)/shard_map/ppermute | solution.py:396
  152.1 14.1 %collective-permute-start.25 = (bf16[400,768]{1,0:T(8,128)(2,1)S(1)}, bf16[400,768]{1,0:T(8,128)(2,1)S(1)}, u32[]{:S(2)}, u32[]{:S(2)}) collective-permute-start(bf16[400,768]{1,0:T(8,128)(2,1)S(1)} %get-tuple-element.52), channel_id=1, source_target_pairs={{0,32},{32,64},{64,96},{96,128},{128,160},{160,192},{192,224},{224... | collective-permute-start | bytes 1843208 | tf_op jit(solution)/shard_map/ppermute | solution.py:396
  152.2 15.3 %collective-permute-start.26 = (bf16[400,768]{1,0:T(8,128)(2,1)S(1)}, bf16[400,768]{1,0:T(8,128)(2,1)S(1)}, u32[]{:S(2)}, u32[]{:S(2)}) collective-permute-start(bf16[400,768]{1,0:T(8,128)(2,1)S(1)} %get-tuple-element.53), channel_id=1, source_target_pairs={{0,224},{32,0},{64,32},{96,64},{128,96},{160,128},{192,160},{224,1... | collective-permute-start | bytes 1843208 | tf_op jit(solution)/shard_map/ppermute | solution.py:396
  202.3 11.4 %collective-permute-start.28 = (bf16[144,768]{1,0:T(8,128)(2,1)S(1)}, bf16[144,768]{1,0:T(8,128)(2,1)S(1)}, u32[]{:S(2)}, u32[]{:S(2)}) collective-permute-start(bf16[144,768]{1,0:T(8,128)(2,1)S(1)} %combine.1.a_ref), channel_id=1, source_target_pairs={{0,2},{1,3},{2,0},{3,1},{4,6},{5,7},{6,4},{7,5},{8,10},{9,11},{10,... | collective-permute-start | bytes 663560 | tf_op jit(solution)/shard_map/ppermute | solution.py:396
  204.4 10.0 %collective-permute-start.29 = (bf16[144,768]{1,0:T(8,128)(2,1)S(1)}, bf16[144,768]{1,0:T(8,128)(2,1)S(1)}, u32[]{:S(2)}, u32[]{:S(2)}) collective-permute-start(bf16[144,768]{1,0:T(8,128)(2,1)S(1)} %combine.1.a_ref), channel_id=1, source_target_pairs={{0,3},{1,0},{2,1},{3,2},{4,7},{5,4},{6,5},{7,6},{8,11},{9,8},{10,9... | collective-permute-start | bytes 663560 | tf_op jit(solution)/shard_map/ppermute | solution.py:396
  (29 other events, 227.7 us)
Sparse Core Ops, SparseCore 0:
  37.4 46.5 all-gather.2
